TPU v7x, 32 devices: a whole 2x2x4 slice. The times are simulated.
32 devices in a mesh: sub: 8 (over z, x), crow: 4 (over y, core).
Axes of the slice: x: 2, y: 2, z: 4, core: 2. Of those that a mesh axis runs over, the one named last changes fastest.
Arguments:
- deflation: bfloat16 [8, 12288, 128], P('sub', 'crow'), as said below
- diag_op: bfloat16 [8, 96, 128, 128], P('sub', 'crow'), as said below
- upper_op: bfloat16 [8, 96, 128, 128], P('sub', 'crow'), may hold values from -0.022094727 to 0.022094727
- tile_blocks: int32 [8, 4, 16], P('sub', 'crow'), may hold values from 0 to 23
- pair_counts: int32 [8, 8], P('sub'), may hold values from 0 to 8, as said below
- pivot_owner: int32 [8], P('sub'), may hold values from 0 to 3
Outputs:
- schur_self: float32 [1024, 128], P(('sub', 'crow'))
- schur_coupling: float32 [1024, 1024], P(('sub', 'crow'))
- panel: float32 [1024, 32], P(('sub', 'crow'))
Inputs may be any that keep to these rules, and one draw needn't show every extreme that they name: deflation has independent columns of different scales. Each diag_op block is symmetric with a positive diagonal, and every A_s is symmetric positive definite. pair_counts[s, j] equals pair_counts[s + o[j], 7 - j], is 0 where s + o[j] lies outside 0 to 7, and the pair of subdomains 0 and 1 shares 8 tiles.
All inputs are finite; a program needn't handle non-finite values.
Results may differ from a plain program's by a relative error of at most 0.0029.
Values may be sent and summed in bfloat16 or wider, within the bound.
A program may use at most 64 MiB of HBM per device.

v0:
```python
import jax
import jax.numpy as jnp
from jax import lax
from jax.sharding import PartitionSpec as P


def padded_2(block, sides, width):
    for axis, dim in sides:
        count = lax.axis_size(axis)
        forward = [(i, i + 1) for i in range(count - 1)]
        backward = [(target, source) for source, target in forward]
        low = lax.ppermute(
            lax.slice_in_dim(block, block.shape[dim] - width, None, axis=dim), axis, forward
        )
        high = lax.ppermute(lax.slice_in_dim(block, 0, width, axis=dim), axis, backward)
        block = jnp.concatenate([low, block, high], axis=dim)
    return block


def shifted(value, axis, steps):
    count = lax.axis_size(axis)
    initial, last = (max(0, -steps), min(count, count - steps))
    return lax.ppermute(value, axis, [(source, source + steps) for source in range(initial, last)])


def broadcast(shard, axis, root):
    mine = lax.axis_index(axis) == root
    return lax.psum(jnp.where(mine, shard, jnp.zeros_like(shard)), axis)


def neighbour_offsets(across):
    return [-across - 1, -across, -across + 1, -1, 1, across - 1, across, across + 1]


def per_device(deflation, diag_op, upper_op, tile_blocks, pair_counts, pivot_owner):
    crow_count = lax.axis_size("crow")
    crow_place = lax.axis_index("crow")
    sub_count = lax.axis_size("sub")
    across = min(16, sub_count // 2)
    offsets = neighbour_offsets(across)
    local_rows = deflation[0]
    blocks_here, tile_rows = (diag_op.shape[1], diag_op.shape[2])
    coarse_width = local_rows.shape[1]
    slot_count = pair_counts.shape[1]
    per_slot = tile_blocks.shape[2] // slot_count
    padded = padded_2(local_rows, (("crow", 0),), tile_rows)
    stacked = padded.reshape(blocks_here + 2, tile_rows, coarse_width)
    centre = stacked[1:-1]
    previous_upper = shifted(upper_op[0, blocks_here - 1], "crow", 1)
    lower_blocks = jnp.concatenate([previous_upper[None], upper_op[0, :-1]], 0)
    product = (
        jnp.einsum("bij,bjk->bik", diag_op[0], centre, preferred_element_type=jnp.float32)
        + jnp.einsum("bij,bjk->bik", upper_op[0], stacked[2:], preferred_element_type=jnp.float32)
        + jnp.einsum("bji,bjk->bik", lower_blocks, stacked[:-2], preferred_element_type=jnp.float32)
    )
    applied = product.astype(jnp.bfloat16)
    chosen = tile_blocks[0, 0]
    own_tiles = centre[chosen].reshape(slot_count, per_slot, tile_rows, coarse_width)
    outgoing = applied[chosen].reshape(slot_count, per_slot, tile_rows, coarse_width)
    position = crow_place * per_slot + jnp.arange(per_slot, dtype=jnp.int32)
    live_mask = (position[None, :] < pair_counts[0][:, None]).astype(jnp.bfloat16)
    own_masked = own_tiles * live_mask[:, :, None, None]
    arrived = [None] * slot_count
    for slot_index in range(slot_count):
        arrived[slot_index] = shifted(
            outgoing[slot_count - 1 - slot_index], "sub", -offsets[slot_index]
        )
    received = jnp.stack(arrived)
    flat_vectors = centre.reshape(blocks_here * tile_rows, coarse_width)
    flat_applied = applied.reshape(blocks_here * tile_rows, coarse_width)
    row_share = coarse_width // crow_count
    owner_index = pivot_owner[0]
    gram_part = jnp.einsum(
        "nr,nk->rk", flat_vectors, flat_applied, preferred_element_type=jnp.float32
    )
    coupling = jnp.einsum(
        "jutr,jutk->rjk", own_masked, received, preferred_element_type=jnp.float32
    )
    own_rows = lax.psum_scatter(
        jnp.concatenate([gram_part[:, None, :], coupling], 1).reshape(
            row_share * lax.axis_size("crow"), (slot_count + 1) * coarse_width
        ),
        "crow",
        scatter_dimension=0,
        tiled=True,
    )
    leading = broadcast(own_rows, "crow", owner_index)
    pivot_block = lax.dynamic_slice_in_dim(leading, owner_index * row_share, row_share, 1)
    factor = jnp.linalg.cholesky(pivot_block)
    solved = jax.scipy.linalg.solve_triangular(factor, leading, lower=True)
    columns = lax.dynamic_slice_in_dim(own_rows, owner_index * row_share, row_share, 1)
    panel_rows = jax.scipy.linalg.solve_triangular(factor, columns.T, lower=True).T
    updated = own_rows - jnp.dot(panel_rows, solved, precision=lax.Precision.HIGHEST)
    return (updated[:, :coarse_width], updated[:, coarse_width:], panel_rows)


def solution(mesh):
    placed = (
        P("sub", "crow", None),
        P("sub", "crow", None, None),
        P("sub", "crow", None, None),
        P("sub", "crow", None),
        P("sub", None),
        P("sub"),
    )
    return jax.shard_map(
        per_device,
        mesh=mesh,
        in_specs=placed,
        out_specs=(P(("sub", "crow"), None), P(("sub", "crow"), None), P(("sub", "crow"), None)),
        check_vma=False,
    )
```

profile of v0, /device:TPU:0, one launch (start us, length us, event | category | flops | bytes accessed | tf_op | source)
XLA Modules:
  0.0 134.4 jit_solution(8377584083666328655)
XLA Ops:
  7.2 0.8 slice_bitcast_fusion
  8.1 1.3 collective-permute-start
  9.4 3.0 %collective-permute-start.2 = (bf16[128,128]{1,0:T(8,128)(2,1)S(1)}, bf16[128,128]{1,0:T(8,128)(2,1)S(1)}, u32[]{:S(2)}, u32[]{:S(2)}) collective-permute-start(bf16[128,128]{1,0:T(8,128)(2,1)S(1)} %get-tuple-element.11), channel_id=1, source_target_pairs={{0,1},{1,2},{2,3},{4,5},{5,6},{6,7},{8,9},{9,10},{10,11},{12,13},{... | collective-permute-start | bytes 98312 | tf_op jit(solution)/shard_map/ppermute | solution.py:12
  12.4 0.8 slice.97
  13.2 0.1 copy.27
  13.3 4.5 %collective-permute-start.1 = (bf16[128,128]{0,1:T(8,128)(2,1)S(1)}, bf16[128,128]{0,1:T(8,128)(2,1)S(1)}, u32[]{:S(2)}, u32[]{:S(2)}) collective-permute-start(bf16[128,128]{0,1:T(8,128)(2,1)S(1)} %bitcast.93), channel_id=1, source_target_pairs={{0,1},{1,2},{2,3},{4,5},{5,6},{6,7},{8,9},{9,10},{10,11},{12,13},{... | collective-permute-start | bytes 98312 | tf_op jit(solution)/shard_map/ppermute | solution.py:23
  17.8 0.7 fusion.18
  18.5 1.6 %fusion.7 = f32[24,128,128]{2,1,0:T(8,128)S(1)} fusion(bf16[24,128,128]{2,1,0:T(8,128)(2,1)} %bitcast.82, bf16[1,24,128,128]{3,2,1,0:T(8,128)(2,1)S(1)} %copy-done), kind=kOutput, calls=%fused_computation.15 | convolution fusion | flops 100663296 | bytes 3145728 | tf_op jit(solution)/shard_map/bij,bjk->bik/dot_general | solution.py:52
  20.1 1.0 slice.98
  21.1 2.3 %copy.28 = bf16[1,23,128,128]{2,3,1,0:T(8,128)(2,1)} copy(bf16[1,23,128,128]{3,2,1,0:T(8,128)(2,1)} %slice.98) | data formatting | bytes 1507328
  23.4 1.4 %gather_fusion.1 = bf16[16,128,128]{2,1,0:T(8,128)(2,1)} fusion(bf16[24,128,128]{2,1,0:T(8,128)(2,1)S(1)} %bitcast.83, s32[1024]{0:T(1024)S(1)} %pad_clamp_fusion), kind=kCustom, calls=%fused_computation.1 | custom fusion | bytes 1048640 | tf_op jit(solution)/shard_map/gather | solution.py:58
  24.9 0.1 pad_maximum_fusion
  25.0 1.0 copy-done.4
  26.0 0.4 fusion.5
  26.4 0.7 copy-done.5
  27.1 1.4 %fusion.1 = bf16[24,128,128]{2,1,0:T(8,128)(2,1)} fusion(f32[24,128,128]{2,1,0:T(8,128)S(1)} %fusion.7, f32[24,128,128]{1,2,0:T(8,128)S(1)} %fusion.5, bf16[24,128,128]{2,1,0:T(8,128)(2,1)S(1)} %bitcast.87, bf16[23,128,128]{1,2,0:T(8,128)(2,1)S(1)} %bitcast.88, bf16[1,128,128]{1,2,0:T(8,128)(2,1)S(1)} %bitcast.92), kind=kOutput, calls=%fused_computation.5 | convolution fusion | flops 102236160 | bytes 5505024 | tf_op jit(solution)/shard_map/bji,bjk->bik/dot_general | solution.py:54
  28.5 1.9 %gather_fusion = bf16[16,128,128]{2,1,0:T(8,128)(2,1)S(1)} fusion(bf16[24,128,128]{2,1,0:T(8,128)(2,1)} %fusion.1, s32[1024]{0:T(1024)S(1)} %pad_clamp_fusion), kind=kCustom, calls=%fused_computation | custom fusion | bytes 1048640 | tf_op jit(solution)/shard_map/gather | solution.py:59
  30.4 5.6 %collective-permute-start.3 = (bf16[2,128,128]{2,1,0:T(8,128)(2,1)S(1)}, bf16[2,128,128]{2,1,0:T(8,128)(2,1)S(1)}, u32[]{:S(2)}, u32[]{:S(2)}) collective-permute-start(bf16[2,128,128]{2,1,0:T(8,128)(2,1)S(1)} %get-tuple-element.20), channel_id=1, source_target_pairs={{0,20},{4,24},{8,28},{1,21},{5,25},{9,29},{2,22},{6,26},{10,30},{3... | collective-permute-start | bytes 196616 | tf_op jit(solution)/shard_map/ppermute | solution.py:23
  36.0 1.3 collective-permute-start.4
  37.3 3.5 %collective-permute-start.5 = (bf16[2,128,128]{2,1,0:T(8,128)(2,1)S(1)}, bf16[2,128,128]{2,1,0:T(8,128)(2,1)S(1)}, u32[]{:S(2)}, u32[]{:S(2)}) collective-permute-start(bf16[2,128,128]{2,1,0:T(8,128)(2,1)S(1)} %get-tuple-element.18), channel_id=1, source_target_pairs={{0,12},{4,16},{8,20},{12,24},{16,28},{1,13},{5,17},{9,21},{13,25},... | collective-permute-start | bytes 196616 | tf_op jit(solution)/shard_map/ppermute | solution.py:23
  40.8 1.3 collective-permute-start.6
  42.1 1.3 collective-permute-start.7
  43.4 0.4 convolution_bitcast_fusion.1
  43.8 1.3 collective-permute-start.8
  45.1 1.3 collective-permute-start.9
  46.4 1.3 collective-permute-start.10
  47.8 0.4 collective-permute-done.7
  48.2 3.0 %collective-permute-done.8 = bf16[2,128,128]{2,1,0:T(8,128)(2,1)S(1)} collective-permute-done((bf16[2,128,128]{2,1,0:T(8,128)(2,1)S(1)}, bf16[2,128,128]{2,1,0:T(8,128)(2,1)S(1)}, u32[]{:S(2)}, u32[]{:S(2)}) %collective-permute-start.8) | collective-permute-done | bytes 65568 | tf_op jit(solution)/shard_map/ppermute | solution.py:23
  51.2 6.7 %collective-permute-done.9 = bf16[2,128,128]{2,1,0:T(8,128)(2,1)S(1)} collective-permute-done((bf16[2,128,128]{2,1,0:T(8,128)(2,1)S(1)}, bf16[2,128,128]{2,1,0:T(8,128)(2,1)S(1)}, u32[]{:S(2)}, u32[]{:S(2)}) %collective-permute-start.9) | collective-permute-done | bytes 65568 | tf_op jit(solution)/shard_map/ppermute | solution.py:23
  57.9 1.5 %collective-permute-done.10 = bf16[2,128,128]{2,1,0:T(8,128)(2,1)S(1)} collective-permute-done((bf16[2,128,128]{2,1,0:T(8,128)(2,1)S(1)}, bf16[2,128,128]{2,1,0:T(8,128)(2,1)S(1)}, u32[]{:S(2)}, u32[]{:S(2)}) %collective-permute-start.10) | collective-permute-done | bytes 65568 | tf_op jit(solution)/shard_map/ppermute | solution.py:23
  59.5 0.4 convolution_bitcast_fusion
  59.9 1.1 copy.25
  61.7 17.4 %reduce-scatter.4.cloned.1.call-done = f32[32,1152]{1,0:T(8,128)} async-done(((f32[128,1152]{1,0:T(8,128)}), f32[32,1152]{1,0:T(8,128)}) %reduce-scatter.4.cloned.1.call-update) | async-done | bytes 147472 | tf_op jit(solution)/shard_map/reduce_scatter | solution.py:79
  79.1 1.2 copy.26
  80.3 0.9 broadcast_select_fusion
  81.2 33.8 %all-reduce.2.cloned.1.call-done = f32[32,1152]{0,1:T(8,128)} async-done(((f32[32,1152]{0,1:T(8,128)}), f32[32,1152]{0,1:T(8,128)}) %all-reduce.2.cloned.1.call-update) | async-done | bytes 147472 | tf_op jit(solution)/shard_map/psum | solution.py:28
  115.0 0.7 constant_dynamic-slice_fusion
  115.8 0.7 fusion.16
  116.5 2.9 %cholesky.16 = f32[32,32]{1,0:T(8,128)S(1)} custom-call(f32[32,32]{1,0:T(8,128)S(1)} %fusion.16), custom_call_target="Cholesky" | custom-call | tf_op jit(solution)/shard_map/jit(cholesky)/cholesky | solution.py:89
  119.4 0.6 compare_reduce_fusion
  120.1 0.7 fusion.11
  120.7 2.4 %custom-call.10 = f32[1,32,32]{1,2,0:T(8,128)S(1)} custom-call(f32[1,32,32]{2,1,0:T(8,128)S(1)} %fusion.11), custom_call_target="InvertDiagBlocksLowerTriangular" | custom-call | tf_op jit(solution)/shard_map/jit(_solve_triangular)/triangular_solve | solution.py:92
  123.2 0.2 fusion.14
  123.4 1.8 %fusion.12 = f32[32,1152]{1,0:T(8,128)S(1)} fusion(f32[32,1152]{0,1:T(8,128)} %all-reduce.2.cloned.1.call-done, f32[1,32,32]{1,2,0:T(8,128)S(1)} %custom-call.10), kind=kOutput, calls=%fused_computation.33 | convolution fusion | flops 14155776 | bytes 299008 | tf_op jit(solution)/shard_map/jit(_solve_triangular)/triangular_solve | solution.py:90
  125.2 0.3 convolution_subtract_fusion
  125.6 0.7 slice.126
  126.2 0.6 slice.125
  126.8 0.7 copy.22
  (42 shorter events, 0.5 us)
Async XLA Ops:
  7.2 11.3 %copy-start = (bf16[1,24,128,128]{3,2,1,0:T(8,128)(2,1)S(1)}, bf16[1,24,128,128]{3,2,1,0:T(8,128)(2,1)}, u32[]{:S(2)}) copy-start(bf16[1,24,128,128]{3,2,1,0:T(8,128)(2,1)} %param.7) | copy-start | bytes 2359300
  7.2 71.9 %reduce-scatter.4.cloned.1.call-start = ((), (), s32[]{:S(2)}) async-start(), calls=%async_computation.2 | async-start | bytes 737280 | tf_op jit(solution)/shard_map/reduce_scatter | solution.py:79
  8.1 16.8 %collective-permute-start = (bf16[128,128]{1,0:T(8,128)(2,1)S(1)}, bf16[128,128]{1,0:T(8,128)(2,1)S(1)}, u32[]{:S(2)}, u32[]{:S(2)}) collective-permute-start(bf16[128,128]{1,0:T(8,128)(2,1)S(1)} %get-tuple-element.12), channel_id=1, source_target_pairs={{1,0},{2,1},{3,2},{5,4},{6,5},{7,6},{9,8},{10,9},{11,10},{13,12},{... | collective-permute-start | bytes 98312 | tf_op jit(solution)/shard_map/ppermute | solution.py:15
  9.4 15.5 %collective-permute-start.2 = (bf16[128,128]{1,0:T(8,128)(2,1)S(1)}, bf16[128,128]{1,0:T(8,128)(2,1)S(1)}, u32[]{:S(2)}, u32[]{:S(2)}) collective-permute-start(bf16[128,128]{1,0:T(8,128)(2,1)S(1)} %get-tuple-element.11), channel_id=1, source_target_pairs={{0,1},{1,2},{2,3},{4,5},{5,6},{6,7},{8,9},{9,10},{10,11},{12,13},{... | collective-permute-start | bytes 98312 | tf_op jit(solution)/shard_map/ppermute | solution.py:12
  13.3 13.1 %collective-permute-start.1 = (bf16[128,128]{0,1:T(8,128)(2,1)S(1)}, bf16[128,128]{0,1:T(8,128)(2,1)S(1)}, u32[]{:S(2)}, u32[]{:S(2)}) collective-permute-start(bf16[128,128]{0,1:T(8,128)(2,1)S(1)} %bitcast.93), channel_id=1, source_target_pairs={{0,1},{1,2},{2,3},{4,5},{5,6},{6,7},{8,9},{9,10},{10,11},{12,13},{... | collective-permute-start | bytes 98312 | tf_op jit(solution)/shard_map/ppermute | solution.py:23
  18.5 1.6 %copy-start.8 = (s32[1,8]{1,0:T(1,128)S(1)}, s32[1,8]{1,0:T(1,128)}, u32[]{:S(2)}) copy-start(s32[1,8]{1,0:T(1,128)} %param.10) | copy-start | bytes 100
  18.5 1.7 %copy-start.3 = (bf16[1,24,128,128]{3,2,1,0:T(8,128)(2,1)S(1)}, bf16[1,24,128,128]{3,2,1,0:T(8,128)(2,1)}, u32[]{:S(2)}) copy-start(bf16[1,24,128,128]{3,2,1,0:T(8,128)(2,1)} %param.8) | copy-start | bytes 2359300
  20.0 3.4 %copy-start.1 = (bf16[1,3072,128]{2,1,0:T(8,128)(2,1)S(1)}, bf16[1,3072,128]{2,1,0:T(8,128)(2,1)}, u32[]{:S(2)}) copy-start(bf16[1,3072,128]{2,1,0:T(8,128)(2,1)} %param.6) | copy-start | bytes 2359300
  24.8 1.1 copy-start.4
  26.0 1.1 copy-start.5
  28.5 14.9 %copy-start.2 = (bf16[24,128,128]{2,1,0:T(8,128)(2,1)S(1)}, bf16[24,128,128]{2,1,0:T(8,128)(2,1)}, u32[]{:S(2)}) copy-start(bf16[24,128,128]{2,1,0:T(8,128)(2,1)} %fusion.1) | copy-start | bytes 2359300
  30.4 29.1 %copy-start.6 = (bf16[16,128,128]{2,1,0:T(8,128)(2,1)S(1)}, bf16[16,128,128]{2,1,0:T(8,128)(2,1)}, u32[]{:S(2)}) copy-start(bf16[16,128,128]{2,1,0:T(8,128)(2,1)} %gather_fusion.1) | copy-start | bytes 1572868
  30.4 13.4 %collective-permute-start.3 = (bf16[2,128,128]{2,1,0:T(8,128)(2,1)S(1)}, bf16[2,128,128]{2,1,0:T(8,128)(2,1)S(1)}, u32[]{:S(2)}, u32[]{:S(2)}) collective-permute-start(bf16[2,128,128]{2,1,0:T(8,128)(2,1)S(1)} %get-tuple-element.20), channel_id=1, source_target_pairs={{0,20},{4,24},{8,28},{1,21},{5,25},{9,29},{2,22},{6,26},{10,30},{3... | collective-permute-start | bytes 196616 | tf_op jit(solution)/shard_map/ppermute | solution.py:23
  36.0 9.1 %collective-permute-start.4 = (bf16[2,128,128]{2,1,0:T(8,128)(2,1)S(1)}, bf16[2,128,128]{2,1,0:T(8,128)(2,1)S(1)}, u32[]{:S(2)}, u32[]{:S(2)}) collective-permute-start(bf16[2,128,128]{2,1,0:T(8,128)(2,1)S(1)} %get-tuple-element.19), channel_id=1, source_target_pairs={{0,16},{4,20},{8,24},{12,28},{1,17},{5,21},{9,25},{13,29},{2,18},{... | collective-permute-start | bytes 196616 | tf_op jit(solution)/shard_map/ppermute | solution.py:23
  37.3 9.2 %collective-permute-start.5 = (bf16[2,128,128]{2,1,0:T(8,128)(2,1)S(1)}, bf16[2,128,128]{2,1,0:T(8,128)(2,1)S(1)}, u32[]{:S(2)}, u32[]{:S(2)}) collective-permute-start(bf16[2,128,128]{2,1,0:T(8,128)(2,1)S(1)} %get-tuple-element.18), channel_id=1, source_target_pairs={{0,12},{4,16},{8,20},{12,24},{16,28},{1,13},{5,17},{9,21},{13,25},... | collective-permute-start | bytes 196616 | tf_op jit(solution)/shard_map/ppermute | solution.py:23
  40.8 7.0 %collective-permute-start.6 = (bf16[2,128,128]{2,1,0:T(8,128)(2,1)S(1)}, bf16[2,128,128]{2,1,0:T(8,128)(2,1)S(1)}, u32[]{:S(2)}, u32[]{:S(2)}) collective-permute-start(bf16[2,128,128]{2,1,0:T(8,128)(2,1)S(1)} %get-tuple-element.17), channel_id=1, source_target_pairs={{0,4},{4,8},{8,12},{12,16},{16,20},{20,24},{24,28},{1,5},{5,9},{9,... | collective-permute-start | bytes 196616 | tf_op jit(solution)/shard_map/ppermute | solution.py:23
  42.1 6.2 %collective-permute-start.7 = (bf16[2,128,128]{2,1,0:T(8,128)(2,1)S(1)}, bf16[2,128,128]{2,1,0:T(8,128)(2,1)S(1)}, u32[]{:S(2)}, u32[]{:S(2)}) collective-permute-start(bf16[2,128,128]{2,1,0:T(8,128)(2,1)S(1)} %get-tuple-element.16), channel_id=1, source_target_pairs={{4,0},{8,4},{12,8},{16,12},{20,16},{24,20},{28,24},{5,1},{9,5},{13... | collective-permute-start | bytes 196616 | tf_op jit(solution)/shard_map/ppermute | solution.py:23
  43.8 7.4 %collective-permute-start.8 = (bf16[2,128,128]{2,1,0:T(8,128)(2,1)S(1)}, bf16[2,128,128]{2,1,0:T(8,128)(2,1)S(1)}, u32[]{:S(2)}, u32[]{:S(2)}) collective-permute-start(bf16[2,128,128]{2,1,0:T(8,128)(2,1)S(1)} %get-tuple-element.15), channel_id=1, source_target_pairs={{12,0},{16,4},{20,8},{24,12},{28,16},{13,1},{17,5},{21,9},{25,13},... | collective-permute-start | bytes 196616 | tf_op jit(solution)/shard_map/ppermute | solution.py:23
  45.1 12.8 %collective-permute-start.9 = (bf16[2,128,128]{2,1,0:T(8,128)(2,1)S(1)}, bf16[2,128,128]{2,1,0:T(8,128)(2,1)S(1)}, u32[]{:S(2)}, u32[]{:S(2)}) collective-permute-start(bf16[2,128,128]{2,1,0:T(8,128)(2,1)S(1)} %get-tuple-element.14), channel_id=1, source_target_pairs={{16,0},{20,4},{24,8},{28,12},{17,1},{21,5},{25,9},{29,13},{18,2},{... | collective-permute-start | bytes 196616 | tf_op jit(solution)/shard_map/ppermute | solution.py:23
  46.4 13.0 %collective-permute-start.10 = (bf16[2,128,128]{2,1,0:T(8,128)(2,1)S(1)}, bf16[2,128,128]{2,1,0:T(8,128)(2,1)S(1)}, u32[]{:S(2)}, u32[]{:S(2)}) collective-permute-start(bf16[2,128,128]{2,1,0:T(8,128)(2,1)S(1)} %get-tuple-element.13), channel_id=1, source_target_pairs={{20,0},{24,4},{28,8},{21,1},{25,5},{29,9},{22,2},{26,6},{30,10},{2... | collective-permute-start | bytes 196616 | tf_op jit(solution)/shard_map/ppermute | solution.py:23
  61.0 54.0 %all-reduce.2.cloned.1.call-start = ((), (), s32[]{:S(2)}) async-start(), calls=%async_computation.1 | async-start | bytes 1179648 | tf_op jit(solution)/shard_map/psum | solution.py:28
  79.1 46.2 %copy-start.7 = (f32[32,1152]{1,0:T(8,128)S(1)}, f32[32,1152]{1,0:T(8,128)}, u32[]{:S(2)}) copy-start(f32[32,1152]{1,0:T(8,128)} %reduce-scatter.4.cloned.1.call-done) | copy-start | bytes 442372
Sparse Core Ops, SparseCore 0:
  61.1 17.9 reduce-scatter.3
  81.4 33.5 all-reduce.1
where the time goes:
time: 135 us; the launch traced here: 134 us
  waiting for transfers between devices  62.8 us (47%)
  starting transfers between devices  25.7 us (19%)
  local copies, waits for them, and re-layouts  15.2 us (11%)
  between operations  15 us (11%)
  other arithmetic  9.15 us (7%)
  matrix products  6.47 us (5%)
    psum x1, waiting for transfers between devices, broadcast(): return lax.psum(jnp.where(mine, shard, jnp.zeros_like(shard)), axis)  33.8 us
    ppermute x9, starting transfers between devices, shifted(): lax.ppermute(value, axis, [(source, source + steps) for source in range(i...  21.3 us
    reduce_scatter x1, waiting for transfers between devices, per_device(): lax.psum_scatter(jnp.concatenate([gram_part[:, None, :], coupling], 1).re...  17.4 us
    ppermute x9, waiting for transfers between devices, shifted(): lax.ppermute(value, axis, [(source, source + steps) for source in range(i...  11.6 us
    unnamed x30, local copies, waits for them, and re-layouts  7.24 us
    another operation x3, other arithmetic, per_device(): factor = jnp.linalg.cholesky(pivot_block)  3.59 us
    another operation x2, other arithmetic, per_device(): jax.scipy.linalg.solve_triangular(factor, columns.T, lower=True)  3.09 us
    ppermute x1, starting transfers between devices, padded_2(): lax.ppermute(lax.slice_in_dim(block, block.shape[dim] - width, None, axis...  3.03 us
  transfers between devices with their start and end apart: 13, of which 6 were waited for; matrix products, arithmetic and copies ran while one was open for 7% of the time, Pallas kernels for 0%

commit v1 on v0

v1 whole, which is shorter than its diff:
```python
import functools

import jax
import jax.numpy as jnp
from jax import lax
from jax.experimental import pallas as pl
from jax.experimental.pallas import tpu as pltpu
from jax.sharding import PartitionSpec as P

MESH = pl.DeviceIdType.MESH
HIGHEST = lax.Precision.HIGHEST
F32 = jnp.float32
BF16 = jnp.bfloat16


def neighbour_offsets(across):
    return [-across - 1, -across, -across + 1, -1, 1, across - 1, across, across + 1]


def dot(a, b, dims=((1,), (0,)), precision=None):
    return lax.dot_general(a, b, (dims, ((), ())), precision=precision, preferred_element_type=F32)


def lanes_from(x, owner, share, parts):
    width = x.shape[1]
    chosen = jnp.broadcast_to(owner, x.shape)
    out = x
    for part in range(1, parts):
        out = jnp.where(chosen == part, pltpu.roll(x, width - part * share, 1), out)
    return out


def kernel(
    offsets, sub_count, crow_count, early,
    z_hbm, d_hbm, u_hbm, tiles, counts, owners,
    self_out, coupling_out, panel_out,
    zbuf, dbuf, ubuf, outgoing, arrived, own, product, reduced, partial, grams, gram, gram_t,
    load_sem, halo_send, halo_recv, tile_send, tile_recv, gram_send, gram_recv, red_send, red_recv,
):
    s = lax.axis_index("sub")
    c = lax.axis_index("crow")
    blocks = dbuf.shape[0]
    rows = dbuf.shape[1]
    width = zbuf.shape[2]
    slots = len(offsets)
    per_slot = outgoing.shape[1] // rows
    share = width // crow_count
    peers = [lax.rem(c + r, crow_count) for r in range(1, crow_count)]
    inside = [jnp.logical_and(s + o >= 0, s + o < sub_count) for o in offsets]
    order = [k for pair in zip(range(slots), reversed(range(slots))) for k in pair][:slots]

    loads = [
        pltpu.make_async_copy(z_hbm, zbuf.at[pl.ds(1, blocks)], load_sem.at[0]),
        pltpu.make_async_copy(d_hbm, dbuf, load_sem.at[1]),
        pltpu.make_async_copy(u_hbm, ubuf.at[pl.ds(1, blocks)], load_sem.at[2]),
    ]
    for load in loads:
        load.start()

    barrier = pltpu.get_barrier_semaphore()
    for peer in peers:
        pl.semaphore_signal(barrier, inc=1, device_id={"crow": peer}, device_id_type=MESH)
    expected = crow_count - 1
    for j in range(slots):
        @pl.when(inside[j])
        def _():
            pl.semaphore_signal(barrier, inc=1, device_id={"sub": s + offsets[j]}, device_id_type=MESH)
        expected = expected + jnp.where(inside[j], 1, 0)
    pl.semaphore_wait(barrier, expected)

    has_left, has_right = c > 0, c < crow_count - 1

    def halo(k):
        source, target, peer = (
            (z_hbm.at[blocks - 1], zbuf.at[0], c + 1),
            (u_hbm.at[blocks - 1], ubuf.at[0], c + 1),
            (z_hbm.at[0], zbuf.at[blocks + 1], c - 1),
        )[k]
        return pltpu.make_async_remote_copy(
            src_ref=source, dst_ref=target, send_sem=halo_send.at[k], recv_sem=halo_recv.at[k],
            device_id={"crow": peer}, device_id_type=MESH,
        )

    @pl.when(has_right)
    def _():
        halo(0).start()
        halo(1).start()

    @pl.when(has_left)
    def _():
        halo(2).start()

    @pl.when(jnp.logical_not(has_left))
    def _():
        zbuf[0] = jnp.zeros((rows, width), BF16)
        ubuf[0] = jnp.zeros((rows, rows), BF16)

    @pl.when(jnp.logical_not(has_right))
    def _():
        zbuf[blocks + 1] = jnp.zeros((rows, width), BF16)

    for load in loads:
        load.wait()

    def applied(b):
        row = jnp.concatenate([dbuf[b], ubuf[b + 1]], axis=1)
        column = jnp.concatenate([zbuf[b + 1], zbuf[b + 2]], axis=0)
        total = dot(row, column) + dot(ubuf[b], zbuf[b], ((0,), (0,)))
        return total.astype(BF16)

    def add_gram(b, total):
        return total + dot(zbuf[b + 1], applied(b), ((0,), (0,)))

    total = lax.fori_loop(1, 1 + early, add_gram, jnp.zeros((width, width), F32), unroll=2)

    @pl.when(has_left)
    def _():
        halo(0).wait_recv()
        halo(1).wait_recv()

    @pl.when(has_right)
    def _():
        halo(2).wait_recv()

    def tile_copy(j):
        return pltpu.make_async_remote_copy(
            src_ref=outgoing.at[j], dst_ref=arrived.at[slots - 1 - j],
            send_sem=tile_send.at[j], recv_sem=tile_recv.at[slots - 1 - j],
            device_id={"sub": s + offsets[j]}, device_id_type=MESH,
        )

    for j in order:
        @pl.when(inside[j])
        def _():
            for u in range(per_slot):
                outgoing[j, u * rows:(u + 1) * rows] = applied(tiles[0, 0, j * per_slot + u])
            tile_copy(j).start()

    total = add_gram(0, add_gram(blocks - 1, total))
    total = lax.fori_loop(1 + early, blocks - 1, add_gram, total, unroll=2)
    grams[0] = total

    def gram_copy(r):
        return pltpu.make_async_remote_copy(
            src_ref=grams.at[0], dst_ref=grams.at[r],
            send_sem=gram_send.at[r - 1], recv_sem=gram_recv.at[r - 1],
            device_id={"crow": peers[r - 1]}, device_id_type=MESH,
        )

    for r in range(1, crow_count):
        gram_copy(r).start()

    for j in order:
        @pl.when(inside[slots - 1 - j])
        def _():
            i = slots - 1 - j
            for u in range(per_slot):
                tile = zbuf[tiles[0, 0, i * per_slot + u] + 1].astype(F32)
                limit = jnp.broadcast_to(counts[0, i], tile.shape)
                tile = jnp.where(limit > c * per_slot + u, tile, 0.0)
                own[i, :, u * rows:(u + 1) * rows] = tile.T.astype(BF16)

    for r in range(1, crow_count):
        gram_copy(r).wait_recv()
    whole = grams[0]
    for r in range(1, crow_count):
        whole = whole + grams[r]
    gram[...] = whole.reshape(gram.shape)
    gram_t[...] = whole.T.reshape(gram.shape)

    owner = owners[0]
    leading = gram[owner]
    symmetric = 0.5 * (leading + gram_t[owner])
    symmetric = lanes_from(symmetric, owner, share, crow_count)
    row_id = lax.broadcasted_iota(jnp.int32, (share, width), 0)
    lane_id = lax.broadcasted_iota(jnp.int32, (share, width), 1)
    unit = (lane_id - share == row_id).astype(F32)
    state = jnp.where(lane_id < share, symmetric, unit)
    for k in range(share):
        scale = lax.rsqrt(state[k:k + 1, k:k + 1])
        pivot_row = state[k:k + 1, :] * scale
        step = jnp.where(row_id[:, :1] > k, state[:, k:k + 1] * scale, 0.0)
        state = jnp.where(row_id == k, pivot_row, state - step * pivot_row)
    inverse = pltpu.roll(state, width - share, 1)[:, :share]

    columns = lanes_from(whole, owner, share, crow_count)[:, :share]
    panel_all = dot(columns, inverse, ((1,), (1,)), HIGHEST)
    weights = dot(panel_all, inverse, ((1,), (0,)), HIGHEST)
    updated = whole - dot(weights, leading, ((1,), (0,)), HIGHEST)
    gram_t[...] = updated.reshape(gram.shape)
    self_out[...] = gram_t[c]
    gram_t[:, :, :share] = panel_all.reshape(crow_count, share, share)
    panel_out[...] = gram_t[c, :, :share]

    def red_copy(i, r):
        return pltpu.make_async_remote_copy(
            src_ref=reduced.at[i, peers[r]],
            dst_ref=partial.at[i, r],
            send_sem=red_send.at[i, r], recv_sem=red_recv.at[i, r],
            device_id={"crow": peers[r]}, device_id_type=MESH,
        )

    for j in order:
        i = slots - 1 - j

        @pl.when(inside[i])
        def _():
            tile_copy(j).wait_recv()
            here = dot(own[i], arrived[i])
            product[...] = here.reshape(product.shape)
            here = here - dot(weights, product[owner], ((1,), (0,)), HIGHEST)
            reduced[i] = here.reshape(product.shape)
            for r in range(crow_count - 1):
                red_copy(i, r).start()

    for j in order:
        i = slots - 1 - j

        @pl.when(inside[i])
        def _():
            result = reduced[i, c]
            for r in range(crow_count - 1):
                red_copy(i, r).wait_recv()
                result = result + partial[i, r]
            coupling_out[:, i * width:(i + 1) * width] = result

        @pl.when(jnp.logical_not(inside[i]))
        def _():
            coupling_out[:, i * width:(i + 1) * width] = jnp.zeros((share, width), F32)

    @pl.when(has_right)
    def _():
        halo(0).wait_send()
        halo(1).wait_send()

    @pl.when(has_left)
    def _():
        halo(2).wait_send()

    for r in range(1, crow_count):
        gram_copy(r).wait_send()
    for j in range(slots):
        @pl.when(inside[j])
        def _():
            tile_copy(j).wait_send()
            for r in range(crow_count - 1):
                red_copy(j, r).wait_send()


def per_device(deflation, diag_op, upper_op, tile_blocks, pair_counts, pivot_owner):
    crow_count = lax.axis_size("crow")
    sub_count = lax.axis_size("sub")
    offsets = neighbour_offsets(min(16, sub_count // 2))
    blocks, rows = diag_op.shape[1], diag_op.shape[2]
    width = deflation.shape[2]
    slots = pair_counts.shape[1]
    per_slot = tile_blocks.shape[2] // slots
    share = width // crow_count
    others = crow_count - 1
    vmem = pl.BlockSpec(memory_space=pltpu.VMEM)
    smem = pl.BlockSpec(memory_space=pltpu.SMEM)
    hbm = pl.BlockSpec(memory_space=pl.ANY)
    dma = pltpu.SemaphoreType.DMA
    return pl.pallas_call(
        functools.partial(kernel, offsets, sub_count, crow_count, 8),
        out_shape=(
            jax.ShapeDtypeStruct((share, width), F32),
            jax.ShapeDtypeStruct((share, slots * width), F32),
            jax.ShapeDtypeStruct((share, share), F32),
        ),
        in_specs=[hbm, hbm, hbm, smem, smem, smem],
        out_specs=(vmem, vmem, vmem),
        scratch_shapes=[
            pltpu.VMEM((blocks + 2, rows, width), BF16),
            pltpu.VMEM((blocks, rows, rows), BF16),
            pltpu.VMEM((blocks + 1, rows, rows), BF16),
            pltpu.VMEM((slots, per_slot * rows, width), BF16),
            pltpu.VMEM((slots, per_slot * rows, width), BF16),
            pltpu.VMEM((slots, width, per_slot * rows), BF16),
            pltpu.VMEM((crow_count, share, width), F32),
            pltpu.VMEM((slots, crow_count, share, width), F32),
            pltpu.VMEM((slots, others, share, width), F32),
            pltpu.VMEM((crow_count, width, width), F32),
            pltpu.VMEM((crow_count, share, width), F32),
            pltpu.VMEM((crow_count, share, width), F32),
            dma((3,)), dma((3,)), dma((3,)),
            dma((slots,)), dma((slots,)),
            dma((others,)), dma((others,)),
            dma((slots, others)), dma((slots, others)),
        ],
        compiler_params=pltpu.CompilerParams(
            collective_id=0, has_side_effects=True, vmem_limit_bytes=24 * 1024 * 1024
        ),
    )(
        deflation.reshape(blocks, rows, width),
        diag_op.reshape(blocks, rows, rows),
        upper_op.reshape(blocks, rows, rows),
        tile_blocks, pair_counts, pivot_owner,
    )


def solution(mesh):
    placed = (
        P("sub", "crow", None),
        P("sub", "crow", None, None),
        P("sub", "crow", None, None),
        P("sub", "crow", None),
        P("sub", None),
        P("sub"),
    )
    return jax.shard_map(
        per_device,
        mesh=mesh,
        in_specs=placed,
        out_specs=(P(("sub", "crow"), None), P(("sub", "crow"), None), P(("sub", "crow"), None)),
        check_vma=False,
    )
```

time: 135 us -> 34.1 us (0.25)
  waiting for transfers between devices: 62.8 us -> 0 us
  Pallas kernels: 0 us -> 26.6 us
  starting transfers between devices: 25.7 us -> 0 us
  between operations: 15 us -> 1.31 us
  local copies, waits for them, and re-layouts: 15.2 us -> 5.92 us
  other arithmetic: 9.15 us -> 0 us
  matrix products: 6.47 us -> 0 us
    psum x1 -> x0, waiting for transfers between devices: 33.8 us -> none  [broadcast(): return lax.psum(jnp.where(mine, shard, jnp.zeros_like(shard)), axis)]
    pallas_call x0 -> x1, Pallas kernels: none -> 26.6 us  [per_device(): pl.pallas_call(functools.partial(kernel, offsets, sub_count, crow_count,...]
    ppermute x11 -> x0, starting transfers between devices: 25.6 us -> none  [the longest x9 21.3 us: shifted(): lax.ppermute(value, axis, [(source, source + steps) for source in range(i...]
    reduce_scatter x1 -> x0, waiting for transfers between devices: 17.4 us -> none  [per_device(): lax.psum_scatter(jnp.concatenate([gram_part[:, None, :], coupling], 1).re...]
    ppermute x11 -> x0, waiting for transfers between devices: 11.6 us -> none  [the longest x9 11.6 us: shifted(): lax.ppermute(value, axis, [(source, source + steps) for source in range(i...]
    another operation x5 -> x0, other arithmetic: 6.68 us -> none  [the longest x3 3.59 us: per_device(): factor = jnp.linalg.cholesky(pivot_block)]
    dot_general x6 -> x0, matrix products: 4.42 us -> none  [the longest x1 1.57 us: per_device(): jnp.einsum('bij,bjk->bik', diag_op[0], centre, preferred_element_type=jnp...]
    slice x6 -> x0, local copies, waits for them, and re-layouts: 3.9 us -> none  [the longest x2 1.27 us: per_device(): return (updated[:, :coarse_width], updated[:, coarse_width:], panel_rows)]
  transfers between devices with their start and end apart: 13 -> 0, of which waited for: 6 -> 0; matrix products, arithmetic and copies ran while one was open for 7% -> 0% of each run, Pallas kernels for 0% -> 0%
where the time goes in v1:
time: 34.1 us; the launch traced here: 33.8 us
  Pallas kernels  26.6 us (78%)
  local copies, waits for them, and re-layouts  5.92 us (17%)
  between operations  1.31 us (4%)
    pallas_call x1, Pallas kernels, per_device(): pl.pallas_call(functools.partial(kernel, offsets, sub_count, crow_count,...  26.6 us
    unnamed x13, local copies, waits for them, and re-layouts  5.92 us

profile of v1, /device:TPU:0, one launch (start us, length us, event | category | flops | bytes accessed | tf_op | source)
XLA Modules:
  0.0 33.8 jit_solution(5867187037743444232)
XLA Ops:
  1.3 0.0 copy-start.3
  1.3 0.0 copy-start.4
  1.3 0.6 %copy-done.3 = s32[1,1,16]{2,1,0:T(1,128)S(1)} copy-done((s32[1,1,16]{2,1,0:T(1,128)S(1)}, s32[1,1,16]{2,1,0:T(1,128)}, u32[]{:S(2)}) %copy-start.3) | copy-done | bytes 88
  1.9 0.0 copy-done.4
  2.0 0.0 copy-start
  2.0 1.1 %copy-done = bf16[1,3072,128]{2,1,0:T(8,128)(2,1)S(1)} copy-done((bf16[1,3072,128]{2,1,0:T(8,128)(2,1)S(1)}, bf16[1,3072,128]{2,1,0:T(8,128)(2,1)}, u32[]{:S(2)}) %copy-start) | copy-done | bytes 786456
  3.1 0.0 copy-start.1
  3.1 1.1 %copy-done.1 = bf16[1,24,128,128]{3,2,1,0:T(8,128)(2,1)S(1)} copy-done((bf16[1,24,128,128]{3,2,1,0:T(8,128)(2,1)S(1)}, bf16[1,24,128,128]{3,2,1,0:T(8,128)(2,1)}, u32[]{:S(2)}) %copy-start.1) | copy-done | bytes 786456
  4.2 0.0 copy-start.2
  4.2 1.1 %copy-done.2 = bf16[1,24,128,128]{3,2,1,0:T(8,128)(2,1)S(1)} copy-done((bf16[1,24,128,128]{3,2,1,0:T(8,128)(2,1)S(1)}, bf16[1,24,128,128]{3,2,1,0:T(8,128)(2,1)}, u32[]{:S(2)}) %copy-start.2) | copy-done | bytes 786456
  5.4 26.6 %shard_map.85 = (f32[32,128]{1,0:T(8,128)S(1)}, f32[32,1024]{1,0:T(8,128)S(1)}, f32[32,32]{1,0:T(8,128)S(1)}) custom-call(bf16[24,128,128]{2,1,0:T(8,128)(2,1)S(1)} %bitcast.3, bf16[24,128,128]{2,1,0:T(8,128)(2,1)S(1)} %bitcast.4, bf16[24,128,128]{2,1,0:T(8,128)(2,1)S(1)} %bitcast.5, s32[1,1,16]{2,1,0:T(1,128)S(1)} %copy-done.3, s32[1,8]{1,0:T(1,128)S(1)} %copy-done.4, ...), custom_call_target="tpu_custom_call" | custom-call | tf_op jit(solution)/shard_map/pallas_call | solution.py:264
  31.9 0.6 %copy.13 = f32[32,128]{1,0:T(8,128)} copy(f32[32,128]{1,0:T(8,128)S(1)} %get-tuple-element.6) | data formatting | bytes 32768
  32.6 0.7 %copy.14 = f32[32,1024]{1,0:T(8,128)} copy(f32[32,1024]{1,0:T(8,128)S(1)} %get-tuple-element.7) | data formatting | bytes 262144
  33.2 0.6 %copy.15 = f32[32,32]{1,0:T(8,128)} copy(f32[32,32]{1,0:T(8,128)S(1)} %get-tuple-element.8) | data formatting | bytes 8192
Async XLA Ops:
  1.3 0.7 %copy-start.3 = (s32[1,1,16]{2,1,0:T(1,128)S(1)}, s32[1,1,16]{2,1,0:T(1,128)}, u32[]{:S(2)}) copy-start(s32[1,1,16]{2,1,0:T(1,128)} %tiles.1) | copy-start | bytes 196
  1.3 0.7 %copy-start.4 = (s32[1,8]{1,0:T(1,128)S(1)}, s32[1,8]{1,0:T(1,128)}, u32[]{:S(2)}) copy-start(s32[1,8]{1,0:T(1,128)} %counts.1) | copy-start | bytes 100
  2.0 1.1 %copy-start = (bf16[1,3072,128]{2,1,0:T(8,128)(2,1)S(1)}, bf16[1,3072,128]{2,1,0:T(8,128)(2,1)}, u32[]{:S(2)}) copy-start(bf16[1,3072,128]{2,1,0:T(8,128)(2,1)} %param.6) | copy-start | bytes 2359300
  3.1 1.1 %copy-start.1 = (bf16[1,24,128,128]{3,2,1,0:T(8,128)(2,1)S(1)}, bf16[1,24,128,128]{3,2,1,0:T(8,128)(2,1)}, u32[]{:S(2)}) copy-start(bf16[1,24,128,128]{3,2,1,0:T(8,128)(2,1)} %param.7) | copy-start | bytes 2359300
  4.2 1.1 %copy-start.2 = (bf16[1,24,128,128]{3,2,1,0:T(8,128)(2,1)S(1)}, bf16[1,24,128,128]{3,2,1,0:T(8,128)(2,1)}, u32[]{:S(2)}) copy-start(bf16[1,24,128,128]{3,2,1,0:T(8,128)(2,1)} %param.8) | copy-start | bytes 2359300

commit v2 on v1

v2 whole, which is shorter than its diff:
```python
import functools

import jax
import jax.numpy as jnp
from jax import lax
from jax.experimental import pallas as pl
from jax.experimental.pallas import tpu as pltpu
from jax.sharding import PartitionSpec as P

MESH = pl.DeviceIdType.MESH
HIGHEST = lax.Precision.HIGHEST
F32 = jnp.float32
BF16 = jnp.bfloat16
VMEM_BYTES = 56 * 1024 * 1024


def neighbour_offsets(across):
    return [-across - 1, -across, -across + 1, -1, 1, across - 1, across, across + 1]


def dot(a, b, dims=((1,), (0,)), precision=None):
    return lax.dot_general(a, b, (dims, ((), ())), precision=precision, preferred_element_type=F32)


def lanes_from(x, owner, share, parts):
    width = x.shape[1]
    chosen = jnp.broadcast_to(owner, x.shape)
    out = x
    for part in range(1, parts):
        out = jnp.where(chosen == part, pltpu.roll(x, width - part * share, 1), out)
    return out


def kernel(
    offsets, sub_count, crow_count,
    z_hbm, d_hbm, u_hbm, tiles, counts, owners,
    self_out, coupling_out, panel_out,
    zbuf, dbuf, ubuf, abuf, outgoing, arrived, own, product, reduced, partial, pivots, square, panels,
    load_sem, halo_send, halo_recv, tile_send, tile_recv, pivot_send, pivot_recv, red_send, red_recv,
):
    s = lax.axis_index("sub")
    c = lax.axis_index("crow")
    blocks = dbuf.shape[0]
    rows = dbuf.shape[1]
    width = zbuf.shape[2]
    slots = len(offsets)
    per_slot = outgoing.shape[1] // rows
    share = width // crow_count
    others = crow_count - 1
    peers = [lax.rem(c + r, crow_count) for r in range(1, crow_count)]
    inside = [jnp.logical_and(s + o >= 0, s + o < sub_count) for o in offsets]
    order = [k for pair in zip(range(slots), reversed(range(slots))) for k in pair][:slots]

    loads = [
        pltpu.make_async_copy(z_hbm, zbuf.at[pl.ds(1, blocks)], load_sem.at[0]),
        pltpu.make_async_copy(d_hbm, dbuf, load_sem.at[1]),
        pltpu.make_async_copy(u_hbm, ubuf.at[pl.ds(1, blocks)], load_sem.at[2]),
    ]
    for load in loads:
        load.start()

    barrier = pltpu.get_barrier_semaphore()
    for peer in peers:
        pl.semaphore_signal(barrier, inc=1, device_id={"crow": peer}, device_id_type=MESH)
    expected = others
    for j in range(slots):
        @pl.when(inside[j])
        def _():
            pl.semaphore_signal(barrier, inc=1, device_id={"sub": s + offsets[j]}, device_id_type=MESH)
        expected = expected + jnp.where(inside[j], 1, 0)
    pl.semaphore_wait(barrier, expected)

    has_left, has_right = c > 0, c < crow_count - 1

    def halo(k):
        source, target, peer = (
            (z_hbm.at[blocks - 1], zbuf.at[0], c + 1),
            (u_hbm.at[blocks - 1], ubuf.at[0], c + 1),
            (z_hbm.at[0], zbuf.at[blocks + 1], c - 1),
        )[k]
        return pltpu.make_async_remote_copy(
            src_ref=source, dst_ref=target, send_sem=halo_send.at[k], recv_sem=halo_recv.at[k],
            device_id={"crow": peer}, device_id_type=MESH,
        )

    @pl.when(has_right)
    def _():
        halo(0).start()
        halo(1).start()

    @pl.when(has_left)
    def _():
        halo(2).start()

    @pl.when(jnp.logical_not(has_left))
    def _():
        zbuf[0] = jnp.zeros((rows, width), BF16)
        ubuf[0] = jnp.zeros((rows, rows), BF16)

    @pl.when(jnp.logical_not(has_right))
    def _():
        zbuf[blocks + 1] = jnp.zeros((rows, width), BF16)

    for load in loads:
        load.wait()

    def apply(b):
        row = jnp.concatenate([dbuf[b], ubuf[b + 1]], axis=1)
        column = jnp.concatenate([zbuf[b + 1], zbuf[b + 2]], axis=0)
        total = dot(row, column) + dot(ubuf[b], zbuf[b], ((0,), (0,)))
        abuf[b] = total.astype(BF16)

    inner = blocks - 2
    chunk = max(n for n in range(1, 12) if inner % n == 0)

    @pl.loop(0, inner // chunk)
    def _(step):
        for k in range(chunk):
            apply(1 + step * chunk + k)

    @pl.when(has_left)
    def _():
        halo(0).wait_recv()
        halo(1).wait_recv()

    @pl.when(has_right)
    def _():
        halo(2).wait_recv()

    apply(0)
    apply(blocks - 1)

    def tile_copy(j):
        return pltpu.make_async_remote_copy(
            src_ref=outgoing.at[j], dst_ref=arrived.at[slots - 1 - j],
            send_sem=tile_send.at[j], recv_sem=tile_recv.at[slots - 1 - j],
            device_id={"sub": s + offsets[j]}, device_id_type=MESH,
        )

    for j in order:
        @pl.when(inside[j])
        def _():
            for u in range(per_slot):
                outgoing[j, u * rows:(u + 1) * rows] = abuf[tiles[0, 0, j * per_slot + u]]
            tile_copy(j).start()

    group = max(n for n in range(1, 9) if blocks % n == 0)
    gram_t = jnp.zeros((width, width), F32)
    for first in range(0, blocks, group):
        left = abuf[first:first + group].reshape(group * rows, width)
        right = zbuf[first + 1:first + 1 + group].reshape(group * rows, width)
        gram_t = gram_t + dot(left, right, ((0,), (0,)))
    square[...] = gram_t.reshape(square.shape)
    owner = owners[0]
    pivots[0] = square[owner]

    def pivot_copy(r):
        return pltpu.make_async_remote_copy(
            src_ref=pivots.at[0], dst_ref=pivots.at[r],
            send_sem=pivot_send.at[r - 1], recv_sem=pivot_recv.at[r - 1],
            device_id={"crow": peers[r - 1]}, device_id_type=MESH,
        )

    for r in range(1, crow_count):
        pivot_copy(r).start()

    gram = gram_t.T
    product[...] = gram.reshape(product.shape)
    gram_pivot = product[owner]
    for j in order:
        i = slots - 1 - j

        @pl.when(inside[i])
        def _():
            for u in range(per_slot):
                tile = zbuf[tiles[0, 0, i * per_slot + u] + 1].astype(F32)
                limit = jnp.broadcast_to(counts[0, i], tile.shape)
                tile = jnp.where(limit > c * per_slot + u, tile, 0.0)
                own[i, :, u * rows:(u + 1) * rows] = tile.T.astype(BF16)

    for r in range(1, crow_count):
        pivot_copy(r).wait_recv()
    columns = pivots[0]
    for r in range(1, crow_count):
        columns = columns + pivots[r]

    turned = lanes_from(columns, owner, share, crow_count)
    state = 0.5 * (turned[:, :share] + turned.T[:share, :])
    row_id = lax.broadcasted_iota(jnp.int32, (share, width), 0)
    for k in range(share):
        factor = jnp.broadcast_to(state[:, k:k + 1], (share, width))
        scale = lax.rsqrt(factor[k:k + 1, :])
        inverse = scale * scale
        panels[k:k + 1, :] = columns[k:k + 1, :] * scale
        pivot_row = state[k:k + 1, :] * inverse[:, :share]
        column_row = columns[k:k + 1, :] * inverse
        state = jnp.where(row_id[:, :share] == k, pivot_row, state - factor[:, :share] * pivot_row)
        columns = jnp.where(row_id == k, column_row, columns - factor * column_row)
    weights = columns.T

    square[:, :, :share] = panels[...].T.reshape(crow_count, share, share)
    panel_out[...] = square[c, :, :share]

    def red_copy(i, r):
        return pltpu.make_async_remote_copy(
            src_ref=reduced.at[i, peers[r]], dst_ref=partial.at[i, r],
            send_sem=red_send.at[i, r], recv_sem=red_recv.at[i, r],
            device_id={"crow": peers[r]}, device_id_type=MESH,
        )

    def scatter(i, part, pivot_rows):
        part = part - dot(weights, pivot_rows, ((1,), (0,)), HIGHEST)
        reduced[i] = part.reshape(product.shape)
        for r in range(others):
            red_copy(i, r).start()

    def gather(i):
        result = reduced[i, c]
        for r in range(others):
            red_copy(i, r).wait_recv()
            result = result + partial[i, r]
        return result

    scatter(slots, gram, gram_pivot)

    for j in order:
        i = slots - 1 - j

        @pl.when(inside[i])
        def _():
            tile_copy(j).wait_recv()
            here = dot(own[i], arrived[i])
            product[...] = here.reshape(product.shape)
            scatter(i, here, product[owner])

    self_out[...] = gather(slots)
    for j in order:
        i = slots - 1 - j

        @pl.when(inside[i])
        def _():
            coupling_out[:, i * width:(i + 1) * width] = gather(i)

        @pl.when(jnp.logical_not(inside[i]))
        def _():
            coupling_out[:, i * width:(i + 1) * width] = jnp.zeros((share, width), F32)

    @pl.when(has_right)
    def _():
        halo(0).wait_send()
        halo(1).wait_send()

    @pl.when(has_left)
    def _():
        halo(2).wait_send()

    for r in range(1, crow_count):
        pivot_copy(r).wait_send()
        red_copy(slots, r - 1).wait_send()
    for j in range(slots):
        @pl.when(inside[j])
        def _():
            tile_copy(j).wait_send()
            for r in range(others):
                red_copy(j, r).wait_send()


def hand_over(a, b, c, a_out, b_out, c_out, sem):
    copies = [
        pltpu.make_async_copy(source, target, sem.at[k])
        for k, (source, target) in enumerate(((b, b_out), (a, a_out), (c, c_out)))
    ]
    for copy in copies:
        copy.start()
    for copy in copies:
        copy.wait()


def per_device(deflation, diag_op, upper_op, tile_blocks, pair_counts, pivot_owner):
    crow_count = lax.axis_size("crow")
    sub_count = lax.axis_size("sub")
    offsets = neighbour_offsets(min(16, sub_count // 2))
    blocks, rows = diag_op.shape[1], diag_op.shape[2]
    width = deflation.shape[2]
    slots = pair_counts.shape[1]
    per_slot = tile_blocks.shape[2] // slots
    share = width // crow_count
    others = crow_count - 1
    vmem = pl.BlockSpec(memory_space=pltpu.VMEM)
    smem = pl.BlockSpec(memory_space=pltpu.SMEM)
    hbm = pl.BlockSpec(memory_space=pltpu.HBM)
    dma = pltpu.SemaphoreType.DMA
    results = pl.pallas_call(
        functools.partial(kernel, offsets, sub_count, crow_count),
        out_shape=(
            jax.ShapeDtypeStruct((share, width), F32),
            jax.ShapeDtypeStruct((share, slots * width), F32),
            jax.ShapeDtypeStruct((share, share), F32),
        ),
        in_specs=[hbm, hbm, hbm, smem, smem, smem],
        out_specs=(vmem, vmem, vmem),
        scratch_shapes=[
            pltpu.VMEM((blocks + 2, rows, width), BF16),
            pltpu.VMEM((blocks, rows, rows), BF16),
            pltpu.VMEM((blocks + 1, rows, rows), BF16),
            pltpu.VMEM((blocks, rows, width), BF16),
            pltpu.VMEM((slots, per_slot * rows, width), BF16),
            pltpu.VMEM((slots, per_slot * rows, width), BF16),
            pltpu.VMEM((slots, width, per_slot * rows), BF16),
            pltpu.VMEM((crow_count, share, width), F32),
            pltpu.VMEM((slots + 1, crow_count, share, width), F32),
            pltpu.VMEM((slots + 1, others, share, width), F32),
            pltpu.VMEM((crow_count, share, width), F32),
            pltpu.VMEM((crow_count, share, width), F32),
            pltpu.VMEM((share, width), F32),
            dma((3,)), dma((3,)), dma((3,)),
            dma((slots,)), dma((slots,)),
            dma((others,)), dma((others,)),
            dma((slots + 1, others)), dma((slots + 1, others)),
        ],
        compiler_params=pltpu.CompilerParams(
            collective_id=0, has_side_effects=True, vmem_limit_bytes=VMEM_BYTES
        ),
    )(
        deflation.reshape(blocks, rows, width),
        diag_op.reshape(blocks, rows, rows),
        upper_op.reshape(blocks, rows, rows),
        tile_blocks, pair_counts, pivot_owner,
    )
    return pl.pallas_call(
        hand_over,
        out_shape=tuple(jax.ShapeDtypeStruct(x.shape, x.dtype) for x in results),
        in_specs=[hbm] * 3,
        out_specs=(hbm,) * 3,
        scratch_shapes=[dma((3,))],
        compiler_params=pltpu.CompilerParams(vmem_limit_bytes=VMEM_BYTES),
    )(*results)


def solution(mesh):
    placed = (
        P("sub", "crow", None),
        P("sub", "crow", None, None),
        P("sub", "crow", None, None),
        P("sub", "crow", None),
        P("sub", None),
        P("sub"),
    )
    return jax.shard_map(
        per_device,
        mesh=mesh,
        in_specs=placed,
        out_specs=(P(("sub", "crow"), None), P(("sub", "crow"), None), P(("sub", "crow"), None)),
        check_vma=False,
    )
```

time: 34.1 us -> 29.7 us (0.87)
  local copies, waits for them, and re-layouts: 5.92 us -> 0 us
  Pallas kernels: 26.6 us -> 28.3 us
    unnamed x13 -> x0, local copies, waits for them, and re-layouts: 5.92 us -> none
    pallas_call x1 -> x2, Pallas kernels: 26.6 us -> 28.3 us  [the longest x1 22.2 us: per_device(): pl.pallas_call(functools.partial(kernel, offsets, sub_count, crow_count),...]
where the time goes in v2:
time: 29.7 us; the launch traced here: 29.5 us
  Pallas kernels  28.3 us (95%)
  between operations  1.29 us (4%)
    pallas_call x1, Pallas kernels, per_device(): pl.pallas_call(functools.partial(kernel, offsets, sub_count, crow_count),...  22.2 us
    pallas_call x1, Pallas kernels, per_device(): pl.pallas_call(hand_over, out_shape=tuple((jax.ShapeDtypeStruct(x.shape,...  6.09 us

profile of v2, /device:TPU:0, one launch (start us, length us, event | category | flops | bytes accessed | tf_op | source)
XLA Modules:
  0.0 29.5 jit_solution(8509824218935820469)
XLA Ops:
  1.3 22.2 %shard_map.85 = (f32[32,128]{1,0:T(8,128)}, f32[32,1024]{1,0:T(8,128)}, f32[32,32]{1,0:T(8,128)}) custom-call(bf16[24,128,128]{2,1,0:T(8,128)(2,1)} %bitcast.3, bf16[24,128,128]{2,1,0:T(8,128)(2,1)} %bitcast.4, bf16[24,128,128]{2,1,0:T(8,128)(2,1)} %bitcast.5, s32[1,1,16]{2,1,0:T(1,128)} %tiles.1, s32[1,8]{1,0:T(1,128)} %counts.1, s32[1]{0:T(128)S(6)} %copy.9.owners), custom_call_target="tpu_custom_call" | custom-call | tf_op jit(solution)/shard_map/pallas_call | solution.py:293
  23.5 6.1 %shard_map.86 = (f32[32,128]{1,0:T(8,128)}, f32[32,1024]{1,0:T(8,128)}, f32[32,32]{1,0:T(8,128)}) custom-call(f32[32,128]{1,0:T(8,128)} %get-tuple-element.6.a, f32[32,1024]{1,0:T(8,128)} %get-tuple-element.7.b, f32[32,32]{1,0:T(8,128)} %get-tuple-element.8.c), custom_call_target="tpu_custom_call" | custom-call | tf_op jit(solution)/shard_map/pallas_call | solution.py:330

commit v3 on v2

--- a/solution.py
+++ b/solution.py
@@ -12,6 +12,7 @@
 F32 = jnp.float32
 BF16 = jnp.bfloat16
 VMEM_BYTES = 56 * 1024 * 1024
+PIVOTS = 4
 
 
 def neighbour_offsets(across):
@@ -108,16 +109,11 @@
         row = jnp.concatenate([dbuf[b], ubuf[b + 1]], axis=1)
         column = jnp.concatenate([zbuf[b + 1], zbuf[b + 2]], axis=0)
         total = dot(row, column) + dot(ubuf[b], zbuf[b], ((0,), (0,)))
-        abuf[b] = total.astype(BF16)
+        return total.astype(BF16)
 
     inner = blocks - 2
     chunk = max(n for n in range(1, 12) if inner % n == 0)
 
-    @pl.loop(0, inner // chunk)
-    def _(step):
-        for k in range(chunk):
-            apply(1 + step * chunk + k)
-
     @pl.when(has_left)
     def _():
         halo(0).wait_recv()
@@ -126,9 +122,6 @@
     @pl.when(has_right)
     def _():
         halo(2).wait_recv()
-
-    apply(0)
-    apply(blocks - 1)
 
     def tile_copy(j):
         return pltpu.make_async_remote_copy(
@@ -141,8 +134,17 @@
         @pl.when(inside[j])
         def _():
             for u in range(per_slot):
-                outgoing[j, u * rows:(u + 1) * rows] = abuf[tiles[0, 0, j * per_slot + u]]
+                outgoing[j, u * rows:(u + 1) * rows] = apply(tiles[0, 0, j * per_slot + u])
             tile_copy(j).start()
+
+    abuf[0] = apply(0)
+    abuf[blocks - 1] = apply(blocks - 1)
+
+    @pl.loop(0, inner // chunk)
+    def _(step):
+        for k in range(chunk):
+            b = 1 + step * chunk + k
+            abuf[b] = apply(b)
 
     group = max(n for n in range(1, 9) if blocks % n == 0)
     gram_t = jnp.zeros((width, width), F32)
@@ -187,15 +189,33 @@
     turned = lanes_from(columns, owner, share, crow_count)
     state = 0.5 * (turned[:, :share] + turned.T[:share, :])
     row_id = lax.broadcasted_iota(jnp.int32, (share, width), 0)
-    for k in range(share):
-        factor = jnp.broadcast_to(state[:, k:k + 1], (share, width))
-        scale = lax.rsqrt(factor[k:k + 1, :])
-        inverse = scale * scale
-        panels[k:k + 1, :] = columns[k:k + 1, :] * scale
-        pivot_row = state[k:k + 1, :] * inverse[:, :share]
-        column_row = columns[k:k + 1, :] * inverse
-        state = jnp.where(row_id[:, :share] == k, pivot_row, state - factor[:, :share] * pivot_row)
-        columns = jnp.where(row_id == k, column_row, columns - factor * column_row)
+    for first in range(0, share, PIVOTS):
+        ids = range(PIVOTS)
+        factors = [
+            jnp.broadcast_to(state[:, first + q:first + q + 1], (share, width)) for q in ids
+        ]
+        small = [[factors[q][first + p:first + p + 1, :] for q in ids] for p in ids]
+        left = [state[first + p:first + p + 1, :] for p in ids]
+        right = [columns[first + p:first + p + 1, :] for p in ids]
+        for q in ids:
+            scale = lax.rsqrt(small[q][q])
+            inverse = scale * scale
+            panels[first + q:first + q + 1, :] = right[q] * scale
+            small[q] = [x * inverse for x in small[q]]
+            left[q] = left[q] * inverse[:, :share]
+            right[q] = right[q] * inverse
+            for p in ids:
+                if p != q:
+                    ratio = small[p][q]
+                    small[p] = [x - ratio * y for x, y in zip(small[p], small[q])]
+                    left[p] = left[p] - ratio[:, :share] * left[q]
+                    right[p] = right[p] - ratio * right[q]
+        for q in ids:
+            state = state - factors[q][:, :share] * left[q]
+            columns = columns - factors[q] * right[q]
+        for q in ids:
+            state = jnp.where(row_id[:, :share] == first + q, left[q], state)
+            columns = jnp.where(row_id == first + q, right[q], columns)
     weights = columns.T
 
     square[:, :, :share] = panels[...].T.reshape(crow_count, share, share)
@@ -265,15 +285,10 @@
                 red_copy(j, r).wait_send()
 
 
-def hand_over(a, b, c, a_out, b_out, c_out, sem):
-    copies = [
-        pltpu.make_async_copy(source, target, sem.at[k])
-        for k, (source, target) in enumerate(((b, b_out), (a, a_out), (c, c_out)))
-    ]
-    for copy in copies:
-        copy.start()
-    for copy in copies:
-        copy.wait()
+def hand_over(a, b, c, a_out, b_out, c_out):
+    a_out[...] = a[...]
+    b_out[...] = b[...]
+    c_out[...] = c[...]
 
 
 def per_device(deflation, diag_op, upper_op, tile_blocks, pair_counts, pivot_owner):
@@ -293,9 +308,9 @@
     results = pl.pallas_call(
         functools.partial(kernel, offsets, sub_count, crow_count),
         out_shape=(
-            jax.ShapeDtypeStruct((share, width), F32),
-            jax.ShapeDtypeStruct((share, slots * width), F32),
-            jax.ShapeDtypeStruct((share, share), F32),
+            pltpu.VMEM((share, width), F32),
+            pltpu.VMEM((share, slots * width), F32),
+            pltpu.VMEM((share, share), F32),
         ),
         in_specs=[hbm, hbm, hbm, smem, smem, smem],
         out_specs=(vmem, vmem, vmem),
@@ -329,11 +344,9 @@
     )
     return pl.pallas_call(
         hand_over,
-        out_shape=tuple(jax.ShapeDtypeStruct(x.shape, x.dtype) for x in results),
-        in_specs=[hbm] * 3,
-        out_specs=(hbm,) * 3,
-        scratch_shapes=[dma((3,))],
-        compiler_params=pltpu.CompilerParams(vmem_limit_bytes=VMEM_BYTES),
+        out_shape=tuple(jax.ShapeDtypeStruct(x.shape, F32) for x in results),
+        in_specs=[vmem] * 3,
+        out_specs=(vmem,) * 3,
     )(*results)
 
 

time: 29.7 us -> 26.8 us (0.902)
  Pallas kernels: 28.3 us -> 23.4 us
  local copies, waits for them, and re-layouts: 0 us -> 1.83 us
    pallas_call x1, Pallas kernels: 6.09 us -> 1.57 us  [per_device(): pl.pallas_call(hand_over, out_shape=tuple((jax.ShapeDtypeStruct(x.shape,...]
    unnamed x0 -> x6, local copies, waits for them, and re-layouts: none -> 1.83 us
    pallas_call x1, Pallas kernels: 22.2 us -> 21.8 us  [per_device(): pl.pallas_call(functools.partial(kernel, offsets, sub_count, crow_count),...]
where the time goes in v3:
time: 26.8 us; the launch traced here: 26.5 us
  Pallas kernels  23.4 us (87%)
  local copies, waits for them, and re-layouts  1.83 us (7%)
  between operations  1.3 us (5%)
    pallas_call x1, Pallas kernels, per_device(): pl.pallas_call(functools.partial(kernel, offsets, sub_count, crow_count),...  21.8 us
    unnamed x6, local copies, waits for them, and re-layouts  1.83 us
    pallas_call x1, Pallas kernels, per_device(): pl.pallas_call(hand_over, out_shape=tuple((jax.ShapeDtypeStruct(x.shape,...  1.57 us

profile of v3, /device:TPU:0, one launch (start us, length us, event | category | flops | bytes accessed | tf_op | source)
XLA Modules:
  0.0 26.5 jit_solution(17480523225591310592)
XLA Ops:
  1.3 21.8 %shard_map.85 = (f32[32,128]{1,0:T(8,128)S(1)}, f32[32,1024]{1,0:T(8,128)S(1)}, f32[32,32]{1,0:T(8,128)S(1)}) custom-call(bf16[24,128,128]{2,1,0:T(8,128)(2,1)} %bitcast.3, bf16[24,128,128]{2,1,0:T(8,128)(2,1)} %bitcast.4, bf16[24,128,128]{2,1,0:T(8,128)(2,1)} %bitcast.5, s32[1,1,16]{2,1,0:T(1,128)} %tiles.1, s32[1,8]{1,0:T(1,128)} %counts.1, s32[1]{0:T(128)S(6)} %copy.9.owners), custom_call_target="tpu_custom_call" | custom-call | tf_op jit(solution)/shard_map/pallas_call | solution.py:308
  23.1 0.0 copy-start
  23.1 0.6 %copy-done = f32[32,1024]{1,0:T(8,128)} copy-done((f32[32,1024]{1,0:T(8,128)}, f32[32,1024]{1,0:T(8,128)S(1)}, u32[]{:S(2)}) %copy-start) | copy-done | bytes 131096
  23.7 0.0 copy-start.1
  23.7 0.6 %copy-done.1 = f32[32,128]{1,0:T(8,128)} copy-done((f32[32,128]{1,0:T(8,128)}, f32[32,128]{1,0:T(8,128)S(1)}, u32[]{:S(2)}) %copy-start.1) | copy-done | bytes 16408
  24.3 0.0 copy-start.2
  24.3 0.6 %copy-done.2 = f32[32,32]{1,0:T(8,128)} copy-done((f32[32,32]{1,0:T(8,128)}, f32[32,32]{1,0:T(8,128)S(1)}, u32[]{:S(2)}) %copy-start.2) | copy-done | bytes 4120
  24.9 1.6 %shard_map.86 = (f32[32,128]{1,0:T(8,128)}, f32[32,1024]{1,0:T(8,128)}, f32[32,32]{1,0:T(8,128)}) custom-call(f32[32,128]{1,0:T(8,128)} %copy-done.1, f32[32,1024]{1,0:T(8,128)} %copy-done, f32[32,32]{1,0:T(8,128)} %copy-done.2), custom_call_target="tpu_custom_call" | custom-call | tf_op jit(solution)/shard_map/pallas_call | solution.py:345
Async XLA Ops:
  23.1 0.6 %copy-start = (f32[32,1024]{1,0:T(8,128)}, f32[32,1024]{1,0:T(8,128)S(1)}, u32[]{:S(2)}) copy-start(f32[32,1024]{1,0:T(8,128)S(1)} %get-tuple-element.7.b) | copy-start | bytes 393220
  23.7 0.6 %copy-start.1 = (f32[32,128]{1,0:T(8,128)}, f32[32,128]{1,0:T(8,128)S(1)}, u32[]{:S(2)}) copy-start(f32[32,128]{1,0:T(8,128)S(1)} %get-tuple-element.6.a) | copy-start | bytes 49156
  24.3 0.6 %copy-start.2 = (f32[32,32]{1,0:T(8,128)}, f32[32,32]{1,0:T(8,128)S(1)}, u32[]{:S(2)}) copy-start(f32[32,32]{1,0:T(8,128)S(1)} %get-tuple-element.8.c) | copy-start | bytes 12292

commit v4 on v3

--- a/solution.py
+++ b/solution.py
@@ -36,7 +36,7 @@
     offsets, sub_count, crow_count,
     z_hbm, d_hbm, u_hbm, tiles, counts, owners,
     self_out, coupling_out, panel_out,
-    zbuf, dbuf, ubuf, abuf, outgoing, arrived, own, product, reduced, partial, pivots, square, panels,
+    zbuf, ztbuf, dbuf, ubuf, abuf, outgoing, arrived, own, product, reduced, partial, pivots, square, panels,
     load_sem, halo_send, halo_recv, tile_send, tile_recv, pivot_send, pivot_recv, red_send, red_recv,
 ):
     s = lax.axis_index("sub")
@@ -45,7 +45,7 @@
     rows = dbuf.shape[1]
     width = zbuf.shape[2]
     slots = len(offsets)
-    per_slot = outgoing.shape[1] // rows
+    per_slot = outgoing.shape[1]
     share = width // crow_count
     others = crow_count - 1
     peers = [lax.rem(c + r, crow_count) for r in range(1, crow_count)]
@@ -105,14 +105,19 @@
     for load in loads:
         load.wait()
 
+    unroll = max(n for n in range(1, 13) if blocks % n == 0)
+
+    @pl.loop(0, blocks // unroll)
+    def _(step):
+        for k in range(unroll):
+            b = 1 + step * unroll + k
+            ztbuf[b] = zbuf[b].T
+
     def apply(b):
-        row = jnp.concatenate([dbuf[b], ubuf[b + 1]], axis=1)
-        column = jnp.concatenate([zbuf[b + 1], zbuf[b + 2]], axis=0)
-        total = dot(row, column) + dot(ubuf[b], zbuf[b], ((0,), (0,)))
+        row = jnp.concatenate([ztbuf[b], ztbuf[b + 1]], axis=1)
+        column = jnp.concatenate([ubuf[b], dbuf[b]], axis=0)
+        total = dot(row, column) + dot(ztbuf[b + 2], ubuf[b + 1], ((1,), (1,)))
         return total.astype(BF16)
-
-    inner = blocks - 2
-    chunk = max(n for n in range(1, 12) if inner % n == 0)
 
     @pl.when(has_left)
     def _():
@@ -122,6 +127,9 @@
     @pl.when(has_right)
     def _():
         halo(2).wait_recv()
+
+    ztbuf[0] = zbuf[0].T
+    ztbuf[blocks + 1] = zbuf[blocks + 1].T
 
     def tile_copy(j):
         return pltpu.make_async_remote_copy(
@@ -134,24 +142,20 @@
         @pl.when(inside[j])
         def _():
             for u in range(per_slot):
-                outgoing[j, u * rows:(u + 1) * rows] = apply(tiles[0, 0, j * per_slot + u])
+                outgoing[j, u] = apply(tiles[0, 0, j * per_slot + u])
             tile_copy(j).start()
 
-    abuf[0] = apply(0)
-    abuf[blocks - 1] = apply(blocks - 1)
-
-    @pl.loop(0, inner // chunk)
+    @pl.loop(0, blocks // unroll)
     def _(step):
-        for k in range(chunk):
-            b = 1 + step * chunk + k
+        for k in range(unroll):
+            b = step * unroll + k
             abuf[b] = apply(b)
 
-    group = max(n for n in range(1, 9) if blocks % n == 0)
     gram_t = jnp.zeros((width, width), F32)
-    for first in range(0, blocks, group):
-        left = abuf[first:first + group].reshape(group * rows, width)
-        right = zbuf[first + 1:first + 1 + group].reshape(group * rows, width)
-        gram_t = gram_t + dot(left, right, ((0,), (0,)))
+    for first in range(0, blocks, unroll):
+        left = jnp.concatenate([abuf[first + k] for k in range(unroll)], axis=1)
+        right = zbuf[first + 1:first + 1 + unroll].reshape(unroll * rows, width)
+        gram_t = gram_t + dot(left, right)
     square[...] = gram_t.reshape(square.shape)
     owner = owners[0]
     pivots[0] = square[owner]
@@ -175,10 +179,10 @@
         @pl.when(inside[i])
         def _():
             for u in range(per_slot):
-                tile = zbuf[tiles[0, 0, i * per_slot + u] + 1].astype(F32)
+                tile = ztbuf[tiles[0, 0, i * per_slot + u] + 1].astype(F32)
                 limit = jnp.broadcast_to(counts[0, i], tile.shape)
                 tile = jnp.where(limit > c * per_slot + u, tile, 0.0)
-                own[i, :, u * rows:(u + 1) * rows] = tile.T.astype(BF16)
+                own[i, :, u * rows:(u + 1) * rows] = tile.astype(BF16)
 
     for r in range(1, crow_count):
         pivot_copy(r).wait_recv()
@@ -249,7 +253,8 @@
         @pl.when(inside[i])
         def _():
             tile_copy(j).wait_recv()
-            here = dot(own[i], arrived[i])
+            far = jnp.concatenate([arrived[i, u] for u in range(per_slot)], axis=1)
+            here = dot(own[i], far, ((1,), (1,)))
             product[...] = here.reshape(product.shape)
             scatter(i, here, product[owner])
 
@@ -285,10 +290,15 @@
                 red_copy(j, r).wait_send()
 
 
-def hand_over(a, b, c, a_out, b_out, c_out):
-    a_out[...] = a[...]
-    b_out[...] = b[...]
-    c_out[...] = c[...]
+def hand_over(a, b, c, a_out, b_out, c_out, sem):
+    copies = [
+        pltpu.make_async_copy(source, target, sem.at[k])
+        for k, (source, target) in enumerate(((b, b_out), (a, a_out), (c, c_out)))
+    ]
+    for copy in copies:
+        copy.start()
+    for copy in copies:
+        copy.wait()
 
 
 def per_device(deflation, diag_op, upper_op, tile_blocks, pair_counts, pivot_owner):
@@ -316,11 +326,12 @@
         out_specs=(vmem, vmem, vmem),
         scratch_shapes=[
             pltpu.VMEM((blocks + 2, rows, width), BF16),
+            pltpu.VMEM((blocks + 2, width, rows), BF16),
             pltpu.VMEM((blocks, rows, rows), BF16),
             pltpu.VMEM((blocks + 1, rows, rows), BF16),
-            pltpu.VMEM((blocks, rows, width), BF16),
-            pltpu.VMEM((slots, per_slot * rows, width), BF16),
-            pltpu.VMEM((slots, per_slot * rows, width), BF16),
+            pltpu.VMEM((blocks, width, rows), BF16),
+            pltpu.VMEM((slots, per_slot, width, rows), BF16),
+            pltpu.VMEM((slots, per_slot, width, rows), BF16),
             pltpu.VMEM((slots, width, per_slot * rows), BF16),
             pltpu.VMEM((crow_count, share, width), F32),
             pltpu.VMEM((slots + 1, crow_count, share, width), F32),
@@ -346,7 +357,9 @@
         hand_over,
         out_shape=tuple(jax.ShapeDtypeStruct(x.shape, F32) for x in results),
         in_specs=[vmem] * 3,
-        out_specs=(vmem,) * 3,
+        out_specs=(hbm,) * 3,
+        scratch_shapes=[dma((3,))],
+        compiler_params=pltpu.CompilerParams(vmem_limit_bytes=2 * 1024 * 1024),
     )(*results)
 
 

time: 26.8 us -> 23.7 us (0.88)
  local copies, waits for them, and re-layouts: 1.83 us -> 0 us
  Pallas kernels: 23.4 us -> 22.2 us
    unnamed x6 -> x0, local copies, waits for them, and re-layouts: 1.83 us -> none
    pallas_call x1, Pallas kernels: 1.57 us -> 0.69 us  [per_device(): pl.pallas_call(hand_over, out_shape=tuple((jax.ShapeDtypeStruct(x.shape,...]
    pallas_call x1, Pallas kernels: 21.8 us -> 21.5 us  [per_device(): pl.pallas_call(functools.partial(kernel, offsets, sub_count, crow_count),...]
where the time goes in v4:
time: 23.7 us; the launch traced here: 23.4 us
  Pallas kernels  22.2 us (94%)
  between operations  1.29 us (5%)
    pallas_call x1, Pallas kernels, per_device(): pl.pallas_call(functools.partial(kernel, offsets, sub_count, crow_count),...  21.5 us
    pallas_call x1, Pallas kernels, per_device(): pl.pallas_call(hand_over, out_shape=tuple((jax.ShapeDtypeStruct(x.shape,...  0.69 us

profile of v4, /device:TPU:0, one launch (start us, length us, event | category | flops | bytes accessed | tf_op | source)
XLA Modules:
  0.0 23.4 jit_solution(3666303308850996492)
XLA Ops:
  1.3 21.5 %shard_map.85 = (f32[32,128]{1,0:T(8,128)S(1)}, f32[32,1024]{1,0:T(8,128)S(1)}, f32[32,32]{1,0:T(8,128)S(1)}) custom-call(bf16[24,128,128]{2,1,0:T(8,128)(2,1)} %bitcast.3, bf16[24,128,128]{2,1,0:T(8,128)(2,1)} %bitcast.4, bf16[24,128,128]{2,1,0:T(8,128)(2,1)} %bitcast.5, s32[1,1,16]{2,1,0:T(1,128)} %tiles.1, s32[1,8]{1,0:T(1,128)} %counts.1, s32[1]{0:T(128)S(6)} %copy.9.owners), custom_call_target="tpu_custom_call" | custom-call | tf_op jit(solution)/shard_map/pallas_call | solution.py:318
  22.8 0.7 %shard_map.86 = (f32[32,128]{1,0:T(8,128)}, f32[32,1024]{1,0:T(8,128)}, f32[32,32]{1,0:T(8,128)}) custom-call(f32[32,128]{1,0:T(8,128)S(1)} %get-tuple-element.6.a, f32[32,1024]{1,0:T(8,128)S(1)} %get-tuple-element.7.b, f32[32,32]{1,0:T(8,128)S(1)} %get-tuple-element.8.c), custom_call_target="tpu_custom_call" | custom-call | tf_op jit(solution)/shard_map/pallas_call | solution.py:356

commit v5 on v4

--- a/solution.py
+++ b/solution.py
@@ -8,7 +8,6 @@
 from jax.sharding import PartitionSpec as P
 
 MESH = pl.DeviceIdType.MESH
-HIGHEST = lax.Precision.HIGHEST
 F32 = jnp.float32
 BF16 = jnp.bfloat16
 VMEM_BYTES = 56 * 1024 * 1024
@@ -30,6 +29,13 @@
     for part in range(1, parts):
         out = jnp.where(chosen == part, pltpu.roll(x, width - part * share, 1), out)
     return out
+
+
+def thirds(x):
+    first = x.astype(BF16)
+    rest = x - first.astype(F32)
+    second = rest.astype(BF16)
+    return first, second, (rest - second.astype(F32)).astype(BF16)
 
 
 def kernel(
@@ -45,17 +51,20 @@
     rows = dbuf.shape[1]
     width = zbuf.shape[2]
     slots = len(offsets)
-    per_slot = outgoing.shape[1]
+    per_slot = outgoing.shape[1] // rows
     share = width // crow_count
     others = crow_count - 1
     peers = [lax.rem(c + r, crow_count) for r in range(1, crow_count)]
     inside = [jnp.logical_and(s + o >= 0, s + o < sub_count) for o in offsets]
     order = [k for pair in zip(range(slots), reversed(range(slots))) for k in pair][:slots]
 
+    half = (blocks + 1) // 2
     loads = [
-        pltpu.make_async_copy(z_hbm, zbuf.at[pl.ds(1, blocks)], load_sem.at[0]),
-        pltpu.make_async_copy(d_hbm, dbuf, load_sem.at[1]),
-        pltpu.make_async_copy(u_hbm, ubuf.at[pl.ds(1, blocks)], load_sem.at[2]),
+        pltpu.make_async_copy(
+            source.at[pl.ds(first, count)], target.at[pl.ds(first + pad, count)], load_sem.at[k, h]
+        )
+        for h, (first, count) in enumerate(((0, half), (half, blocks - half)))
+        for k, (source, target, pad) in enumerate(((z_hbm, zbuf, 1), (u_hbm, ubuf, 1), (d_hbm, dbuf, 0)))
     ]
     for load in loads:
         load.start()
@@ -106,14 +115,16 @@
         load.wait()
 
     unroll = max(n for n in range(1, 13) if blocks % n == 0)
-
-    @pl.loop(0, blocks // unroll)
-    def _(step):
-        for k in range(unroll):
-            b = 1 + step * unroll + k
-            ztbuf[b] = zbuf[b].T
+    for k in range(unroll):
+        ztbuf[1 + k] = zbuf[1 + k].T
 
     def apply(b):
+        row = jnp.concatenate([dbuf[b], ubuf[b + 1]], axis=1)
+        column = jnp.concatenate([zbuf[b + 1], zbuf[b + 2]], axis=0)
+        total = dot(row, column) + dot(ubuf[b], zbuf[b], ((0,), (0,)))
+        return total.astype(BF16)
+
+    def apply_t(b):
         row = jnp.concatenate([ztbuf[b], ztbuf[b + 1]], axis=1)
         column = jnp.concatenate([ubuf[b], dbuf[b]], axis=0)
         total = dot(row, column) + dot(ztbuf[b + 2], ubuf[b + 1], ((1,), (1,)))
@@ -127,9 +138,6 @@
     @pl.when(has_right)
     def _():
         halo(2).wait_recv()
-
-    ztbuf[0] = zbuf[0].T
-    ztbuf[blocks + 1] = zbuf[blocks + 1].T
 
     def tile_copy(j):
         return pltpu.make_async_remote_copy(
@@ -142,14 +150,23 @@
         @pl.when(inside[j])
         def _():
             for u in range(per_slot):
-                outgoing[j, u] = apply(tiles[0, 0, j * per_slot + u])
+                outgoing[j, u * rows:(u + 1) * rows] = apply(tiles[0, 0, j * per_slot + u])
             tile_copy(j).start()
+
+    @pl.loop(1, blocks // unroll)
+    def _(step):
+        for k in range(unroll):
+            b = 1 + step * unroll + k
+            ztbuf[b] = zbuf[b].T
+
+    ztbuf[0] = zbuf[0].T
+    ztbuf[blocks + 1] = zbuf[blocks + 1].T
 
     @pl.loop(0, blocks // unroll)
     def _(step):
         for k in range(unroll):
             b = step * unroll + k
-            abuf[b] = apply(b)
+            abuf[b] = apply_t(b)
 
     gram_t = jnp.zeros((width, width), F32)
     for first in range(0, blocks, unroll):
@@ -221,6 +238,8 @@
             state = jnp.where(row_id[:, :share] == first + q, left[q], state)
             columns = jnp.where(row_id == first + q, right[q], columns)
     weights = columns.T
+    w0, w1, w2 = thirds(weights)
+    wide = jnp.concatenate([w0, w0, w1, w1, w0, w2], axis=1)
 
     square[:, :, :share] = panels[...].T.reshape(crow_count, share, share)
     panel_out[...] = square[c, :, :share]
@@ -233,7 +252,8 @@
         )
 
     def scatter(i, part, pivot_rows):
-        part = part - dot(weights, pivot_rows, ((1,), (0,)), HIGHEST)
+        p0, p1, p2 = thirds(pivot_rows)
+        part = part - dot(wide, jnp.concatenate([p0, p1, p0, p1, p2, p0], axis=0))
         reduced[i] = part.reshape(product.shape)
         for r in range(others):
             red_copy(i, r).start()
@@ -253,8 +273,7 @@
         @pl.when(inside[i])
         def _():
             tile_copy(j).wait_recv()
-            far = jnp.concatenate([arrived[i, u] for u in range(per_slot)], axis=1)
-            here = dot(own[i], far, ((1,), (1,)))
+            here = dot(own[i], arrived[i])
             product[...] = here.reshape(product.shape)
             scatter(i, here, product[owner])
 
@@ -330,8 +349,8 @@
             pltpu.VMEM((blocks, rows, rows), BF16),
             pltpu.VMEM((blocks + 1, rows, rows), BF16),
             pltpu.VMEM((blocks, width, rows), BF16),
-            pltpu.VMEM((slots, per_slot, width, rows), BF16),
-            pltpu.VMEM((slots, per_slot, width, rows), BF16),
+            pltpu.VMEM((slots, per_slot * rows, width), BF16),
+            pltpu.VMEM((slots, per_slot * rows, width), BF16),
             pltpu.VMEM((slots, width, per_slot * rows), BF16),
             pltpu.VMEM((crow_count, share, width), F32),
             pltpu.VMEM((slots + 1, crow_count, share, width), F32),
@@ -339,7 +358,7 @@
             pltpu.VMEM((crow_count, share, width), F32),
             pltpu.VMEM((crow_count, share, width), F32),
             pltpu.VMEM((share, width), F32),
-            dma((3,)), dma((3,)), dma((3,)),
+            dma((3, 2)), dma((3,)), dma((3,)),
             dma((slots,)), dma((slots,)),
             dma((others,)), dma((others,)),
             dma((slots + 1, others)), dma((slots + 1, others)),

time: 23.7 us -> 24 us (1.013)
  no operation moved by 1% of the time
where the time goes in v5:
time: 24 us; the launch traced here: 23.7 us
  Pallas kernels  22.4 us (93%)
  between operations  1.29 us (5%)
    pallas_call x1, Pallas kernels, per_device(): pl.pallas_call(functools.partial(kernel, offsets, sub_count, crow_count),...  21.7 us
    pallas_call x1, Pallas kernels, per_device(): pl.pallas_call(hand_over, out_shape=tuple((jax.ShapeDtypeStruct(x.shape,...  0.69 us

profile of v5, /device:TPU:0, one launch (start us, length us, event | category | flops | bytes accessed | tf_op | source)
XLA Modules:
  0.0 23.7 jit_solution(8851071916136061298)
XLA Ops:
  1.3 21.7 %shard_map.85 = (f32[32,128]{1,0:T(8,128)S(1)}, f32[32,1024]{1,0:T(8,128)S(1)}, f32[32,32]{1,0:T(8,128)S(1)}) custom-call(bf16[24,128,128]{2,1,0:T(8,128)(2,1)} %bitcast.3, bf16[24,128,128]{2,1,0:T(8,128)(2,1)} %bitcast.4, bf16[24,128,128]{2,1,0:T(8,128)(2,1)} %bitcast.5, s32[1,1,16]{2,1,0:T(1,128)} %tiles.1, s32[1,8]{1,0:T(1,128)} %counts.1, s32[1]{0:T(128)S(6)} %copy.9.owners), custom_call_target="tpu_custom_call" | custom-call | tf_op jit(solution)/shard_map/pallas_call | solution.py:337
  23.0 0.7 %shard_map.86 = (f32[32,128]{1,0:T(8,128)}, f32[32,1024]{1,0:T(8,128)}, f32[32,32]{1,0:T(8,128)}) custom-call(f32[32,128]{1,0:T(8,128)S(1)} %get-tuple-element.6.a, f32[32,1024]{1,0:T(8,128)S(1)} %get-tuple-element.7.b, f32[32,32]{1,0:T(8,128)S(1)} %get-tuple-element.8.c), custom_call_target="tpu_custom_call" | custom-call | tf_op jit(solution)/shard_map/pallas_call | solution.py:375

commit v6 on v5

--- a/solution.py
+++ b/solution.py
@@ -42,8 +42,8 @@
     offsets, sub_count, crow_count,
     z_hbm, d_hbm, u_hbm, tiles, counts, owners,
     self_out, coupling_out, panel_out,
-    zbuf, ztbuf, dbuf, ubuf, abuf, outgoing, arrived, own, product, reduced, partial, pivots, square, panels,
-    load_sem, halo_send, halo_recv, tile_send, tile_recv, pivot_send, pivot_recv, red_send, red_recv,
+    zbuf, ztbuf, dbuf, ubuf, abuf, outgoing, arrived, own, product, reduced, from_core, summed, from_far, pivots, square, panels,
+    load_sem, halo_send, halo_recv, tile_send, tile_recv, pivot_send, pivot_recv, core_send, core_recv, far_send, far_recv,
 ):
     s = lax.axis_index("sub")
     c = lax.axis_index("crow")
@@ -244,26 +244,37 @@
     square[:, :, :share] = panels[...].T.reshape(crow_count, share, share)
     panel_out[...] = square[c, :, :share]
 
-    def red_copy(i, r):
+    half_place, pair_place = lax.rem(c, 2), lax.div(c, 2)
+
+    def core_copy(i):
         return pltpu.make_async_remote_copy(
-            src_ref=reduced.at[i, peers[r]], dst_ref=partial.at[i, r],
-            send_sem=red_send.at[i, r], recv_sem=red_recv.at[i, r],
-            device_id={"crow": peers[r]}, device_id_type=MESH,
+            src_ref=reduced.at[i, 1 - half_place], dst_ref=from_core.at[i],
+            send_sem=core_send.at[i], recv_sem=core_recv.at[i],
+            device_id={"crow": c + 1 - 2 * half_place}, device_id_type=MESH,
+        )
+
+    def far_copy(i):
+        return pltpu.make_async_remote_copy(
+            src_ref=summed.at[i, 1 - pair_place], dst_ref=from_far.at[i],
+            send_sem=far_send.at[i], recv_sem=far_recv.at[i],
+            device_id={"crow": c + 2 - 4 * pair_place}, device_id_type=MESH,
         )
 
     def scatter(i, part, pivot_rows):
         p0, p1, p2 = thirds(pivot_rows)
         part = part - dot(wide, jnp.concatenate([p0, p1, p0, p1, p2, p0], axis=0))
-        reduced[i] = part.reshape(product.shape)
-        for r in range(others):
-            red_copy(i, r).start()
+        for place in range(crow_count):
+            reduced[i, place % 2, place // 2] = part[place * share:(place + 1) * share]
+        core_copy(i).start()
+
+    def pass_on(i):
+        core_copy(i).wait_recv()
+        summed[i] = reduced[i, half_place] + from_core[i]
+        far_copy(i).start()
 
     def gather(i):
-        result = reduced[i, c]
-        for r in range(others):
-            red_copy(i, r).wait_recv()
-            result = result + partial[i, r]
-        return result
+        far_copy(i).wait_recv()
+        return summed[i, pair_place] + from_far[i]
 
     scatter(slots, gram, gram_pivot)
 
@@ -277,6 +288,12 @@
             product[...] = here.reshape(product.shape)
             scatter(i, here, product[owner])
 
+    pass_on(slots)
+    for j in order:
+        @pl.when(inside[slots - 1 - j])
+        def _():
+            pass_on(slots - 1 - j)
+
     self_out[...] = gather(slots)
     for j in order:
         i = slots - 1 - j
@@ -300,13 +317,14 @@
 
     for r in range(1, crow_count):
         pivot_copy(r).wait_send()
-        red_copy(slots, r - 1).wait_send()
+    core_copy(slots).wait_send()
+    far_copy(slots).wait_send()
     for j in range(slots):
         @pl.when(inside[j])
         def _():
             tile_copy(j).wait_send()
-            for r in range(others):
-                red_copy(j, r).wait_send()
+            core_copy(j).wait_send()
+            far_copy(j).wait_send()
 
 
 def hand_over(a, b, c, a_out, b_out, c_out, sem):
@@ -353,15 +371,17 @@
             pltpu.VMEM((slots, per_slot * rows, width), BF16),
             pltpu.VMEM((slots, width, per_slot * rows), BF16),
             pltpu.VMEM((crow_count, share, width), F32),
-            pltpu.VMEM((slots + 1, crow_count, share, width), F32),
-            pltpu.VMEM((slots + 1, others, share, width), F32),
+            pltpu.VMEM((slots + 1, 2, 2, share, width), F32),
+            pltpu.VMEM((slots + 1, 2, share, width), F32),
+            pltpu.VMEM((slots + 1, 2, share, width), F32),
+            pltpu.VMEM((slots + 1, share, width), F32),
             pltpu.VMEM((crow_count, share, width), F32),
             pltpu.VMEM((crow_count, share, width), F32),
             pltpu.VMEM((share, width), F32),
             dma((3, 2)), dma((3,)), dma((3,)),
             dma((slots,)), dma((slots,)),
             dma((others,)), dma((others,)),
-            dma((slots + 1, others)), dma((slots + 1, others)),
+            dma((slots + 1,)), dma((slots + 1,)), dma((slots + 1,)), dma((slots + 1,)),
         ],
         compiler_params=pltpu.CompilerParams(
             collective_id=0, has_side_effects=True, vmem_limit_bytes=VMEM_BYTES

time: 24 us -> 23.8 us (level)
  no operation moved by 1% of the time
where the time goes in v6:
time: 23.8 us; the launch traced here: 23.5 us
  Pallas kernels  22.3 us (94%)
  between operations  1.29 us (5%)
    pallas_call x1, Pallas kernels, per_device(): pl.pallas_call(functools.partial(kernel, offsets, sub_count, crow_count),...  21.6 us
    pallas_call x1, Pallas kernels, per_device(): pl.pallas_call(hand_over, out_shape=tuple((jax.ShapeDtypeStruct(x.shape,...  0.69 us

profile of v6, /device:TPU:0, one launch (start us, length us, event | category | flops | bytes accessed | tf_op | source)
XLA Modules:
  0.0 23.5 jit_solution(11142951955943606135)
XLA Ops:
  1.3 21.6 %shard_map.85 = (f32[32,128]{1,0:T(8,128)S(1)}, f32[32,1024]{1,0:T(8,128)S(1)}, f32[32,32]{1,0:T(8,128)S(1)}) custom-call(bf16[24,128,128]{2,1,0:T(8,128)(2,1)} %bitcast.3, bf16[24,128,128]{2,1,0:T(8,128)(2,1)} %bitcast.4, bf16[24,128,128]{2,1,0:T(8,128)(2,1)} %bitcast.5, s32[1,1,16]{2,1,0:T(1,128)} %tiles.1, s32[1,8]{1,0:T(1,128)} %counts.1, s32[1]{0:T(128)S(6)} %copy.9.owners), custom_call_target="tpu_custom_call" | custom-call | tf_op jit(solution)/shard_map/pallas_call | solution.py:355
  22.8 0.7 %shard_map.86 = (f32[32,128]{1,0:T(8,128)}, f32[32,1024]{1,0:T(8,128)}, f32[32,32]{1,0:T(8,128)}) custom-call(f32[32,128]{1,0:T(8,128)S(1)} %get-tuple-element.6.a, f32[32,1024]{1,0:T(8,128)S(1)} %get-tuple-element.7.b, f32[32,32]{1,0:T(8,128)S(1)} %get-tuple-element.8.c), custom_call_target="tpu_custom_call" | custom-call | tf_op jit(solution)/shard_map/pallas_call | solution.py:395

commit v7 on v6

--- a/solution.py
+++ b/solution.py
@@ -66,9 +66,6 @@
         for h, (first, count) in enumerate(((0, half), (half, blocks - half)))
         for k, (source, target, pad) in enumerate(((z_hbm, zbuf, 1), (u_hbm, ubuf, 1), (d_hbm, dbuf, 0)))
     ]
-    for load in loads:
-        load.start()
-
     barrier = pltpu.get_barrier_semaphore()
     for peer in peers:
         pl.semaphore_signal(barrier, inc=1, device_id={"crow": peer}, device_id_type=MESH)
@@ -78,6 +75,8 @@
         def _():
             pl.semaphore_signal(barrier, inc=1, device_id={"sub": s + offsets[j]}, device_id_type=MESH)
         expected = expected + jnp.where(inside[j], 1, 0)
+    for load in loads:
+        load.start()
     pl.semaphore_wait(barrier, expected)
 
     has_left, has_right = c > 0, c < crow_count - 1
@@ -139,10 +138,11 @@
     def _():
         halo(2).wait_recv()
 
-    def tile_copy(j):
+    def tile_copy(j, u):
+        here = pl.ds(u * rows, rows)
         return pltpu.make_async_remote_copy(
-            src_ref=outgoing.at[j], dst_ref=arrived.at[slots - 1 - j],
-            send_sem=tile_send.at[j], recv_sem=tile_recv.at[slots - 1 - j],
+            src_ref=outgoing.at[j, here], dst_ref=arrived.at[slots - 1 - j, here],
+            send_sem=tile_send.at[j, u], recv_sem=tile_recv.at[slots - 1 - j, u],
             device_id={"sub": s + offsets[j]}, device_id_type=MESH,
         )
 
@@ -151,7 +151,7 @@
         def _():
             for u in range(per_slot):
                 outgoing[j, u * rows:(u + 1) * rows] = apply(tiles[0, 0, j * per_slot + u])
-            tile_copy(j).start()
+                tile_copy(j, u).start()
 
     @pl.loop(1, blocks // unroll)
     def _(step):
@@ -278,18 +278,19 @@
 
     scatter(slots, gram, gram_pivot)
 
-    for j in order:
+    for j in order[::-1]:
         i = slots - 1 - j
 
         @pl.when(inside[i])
         def _():
-            tile_copy(j).wait_recv()
+            for u in range(per_slot):
+                tile_copy(j, u).wait_recv()
             here = dot(own[i], arrived[i])
             product[...] = here.reshape(product.shape)
             scatter(i, here, product[owner])
 
     pass_on(slots)
-    for j in order:
+    for j in order[::-1]:
         @pl.when(inside[slots - 1 - j])
         def _():
             pass_on(slots - 1 - j)
@@ -322,7 +323,8 @@
     for j in range(slots):
         @pl.when(inside[j])
         def _():
-            tile_copy(j).wait_send()
+            for u in range(per_slot):
+                tile_copy(j, u).wait_send()
             core_copy(j).wait_send()
             far_copy(j).wait_send()
 
@@ -379,7 +381,7 @@
             pltpu.VMEM((crow_count, share, width), F32),
             pltpu.VMEM((share, width), F32),
             dma((3, 2)), dma((3,)), dma((3,)),
-            dma((slots,)), dma((slots,)),
+            dma((slots, per_slot)), dma((slots, per_slot)),
             dma((others,)), dma((others,)),
             dma((slots + 1,)), dma((slots + 1,)), dma((slots + 1,)), dma((slots + 1,)),
         ],

time: 23.8 us -> 25 us (1.050)
  the two profiles are of different devices: /device:TPU:0 before, /device:TPU:16 now
where the time goes in v7:
time: 25 us; the launch traced here: 24.8 us
  Pallas kernels  23.6 us (94%)
  between operations  1.29 us (5%)
    pallas_call x1, Pallas kernels, per_device(): pl.pallas_call(functools.partial(kernel, offsets, sub_count, crow_count),...  22.9 us
    pallas_call x1, Pallas kernels, per_device(): pl.pallas_call(hand_over, out_shape=tuple((jax.ShapeDtypeStruct(x.shape,...  0.69 us

profile of v7, /device:TPU:16, one launch (start us, length us, event | category | flops | bytes accessed | tf_op | source)
XLA Modules:
  0.0 24.8 jit_solution(9689941380960000459)
XLA Ops:
  1.3 22.9 %shard_map.85 = (f32[32,128]{1,0:T(8,128)S(1)}, f32[32,1024]{1,0:T(8,128)S(1)}, f32[32,32]{1,0:T(8,128)S(1)}) custom-call(bf16[24,128,128]{2,1,0:T(8,128)(2,1)} %bitcast.3, bf16[24,128,128]{2,1,0:T(8,128)(2,1)} %bitcast.4, bf16[24,128,128]{2,1,0:T(8,128)(2,1)} %bitcast.5, s32[1,1,16]{2,1,0:T(1,128)} %tiles.1, s32[1,8]{1,0:T(1,128)} %counts.1, s32[1]{0:T(128)S(6)} %copy.9.owners), custom_call_target="tpu_custom_call" | custom-call | tf_op jit(solution)/shard_map/pallas_call | solution.py:357
  24.1 0.7 %shard_map.86 = (f32[32,128]{1,0:T(8,128)}, f32[32,1024]{1,0:T(8,128)}, f32[32,32]{1,0:T(8,128)}) custom-call(f32[32,128]{1,0:T(8,128)S(1)} %get-tuple-element.6.a, f32[32,1024]{1,0:T(8,128)S(1)} %get-tuple-element.7.b, f32[32,32]{1,0:T(8,128)S(1)} %get-tuple-element.8.c), custom_call_target="tpu_custom_call" | custom-call | tf_op jit(solution)/shard_map/pallas_call | solution.py:397

commit v8 on v6

--- a/solution.py
+++ b/solution.py
@@ -66,9 +66,6 @@
         for h, (first, count) in enumerate(((0, half), (half, blocks - half)))
         for k, (source, target, pad) in enumerate(((z_hbm, zbuf, 1), (u_hbm, ubuf, 1), (d_hbm, dbuf, 0)))
     ]
-    for load in loads:
-        load.start()
-
     barrier = pltpu.get_barrier_semaphore()
     for peer in peers:
         pl.semaphore_signal(barrier, inc=1, device_id={"crow": peer}, device_id_type=MESH)
@@ -78,6 +75,8 @@
         def _():
             pl.semaphore_signal(barrier, inc=1, device_id={"sub": s + offsets[j]}, device_id_type=MESH)
         expected = expected + jnp.where(inside[j], 1, 0)
+    for load in loads:
+        load.start()
     pl.semaphore_wait(barrier, expected)
 
     has_left, has_right = c > 0, c < crow_count - 1

time: 23.8 us -> 23.8 us (level)
  no operation moved by 1% of the time
where the time goes in v8:
time: 23.8 us; the launch traced here: 23.5 us
  Pallas kernels  22.2 us (93%)
  between operations  1.29 us (5%)
    pallas_call x1, Pallas kernels, per_device(): pl.pallas_call(functools.partial(kernel, offsets, sub_count, crow_count),...  21.6 us
    pallas_call x1, Pallas kernels, per_device(): pl.pallas_call(hand_over, out_shape=tuple((jax.ShapeDtypeStruct(x.shape,...  0.69 us

profile of v8, /device:TPU:0, one launch (start us, length us, event | category | flops | bytes accessed | tf_op | source)
XLA Modules:
  0.0 23.5 jit_solution(16391342521861015038)
XLA Ops:
  1.3 21.6 %shard_map.85 = (f32[32,128]{1,0:T(8,128)S(1)}, f32[32,1024]{1,0:T(8,128)S(1)}, f32[32,32]{1,0:T(8,128)S(1)}) custom-call(bf16[24,128,128]{2,1,0:T(8,128)(2,1)} %bitcast.3, bf16[24,128,128]{2,1,0:T(8,128)(2,1)} %bitcast.4, bf16[24,128,128]{2,1,0:T(8,128)(2,1)} %bitcast.5, s32[1,1,16]{2,1,0:T(1,128)} %tiles.1, s32[1,8]{1,0:T(1,128)} %counts.1, s32[1]{0:T(128)S(6)} %copy.9.owners), custom_call_target="tpu_custom_call" | custom-call | tf_op jit(solution)/shard_map/pallas_call | solution.py:354
  22.8 0.7 %shard_map.86 = (f32[32,128]{1,0:T(8,128)}, f32[32,1024]{1,0:T(8,128)}, f32[32,32]{1,0:T(8,128)}) custom-call(f32[32,128]{1,0:T(8,128)S(1)} %get-tuple-element.6.a, f32[32,1024]{1,0:T(8,128)S(1)} %get-tuple-element.7.b, f32[32,32]{1,0:T(8,128)S(1)} %get-tuple-element.8.c), custom_call_target="tpu_custom_call" | custom-call | tf_op jit(solution)/shard_map/pallas_call | solution.py:394
